TPU v7x, 128 devices: a whole 4x4x4 slice. The times are simulated.
128 devices in a mesh: blk: 64 (over x, y_hi, z, core), rhs: 2 (over y_lo).
Axes of the slice: x: 4, y: 4 (y_hi: 2, y_lo: 2; y = y_hi * 2 + y_lo), z: 4, core: 2. Of those that a mesh axis runs over, the one named last changes fastest.
Arguments:
- rhs_vectors: float32 [64, 1048576], P('rhs', 'blk'), may hold values from -6 to 6
- leaf_basis: bfloat16 [8192, 32, 128], P('blk'), may hold values from -0.5 to 0.5
- leaf_expand: bfloat16 [8192, 32, 128], P(('blk', 'rhs')), may hold values from -1 to 1
- outer_levels: bfloat16 [7, 8192, 2048], P(None, 'blk'), may hold values from -0.75 to 0.75
- inner_levels: bfloat16 [6, 8192, 2048], P(None, ('blk', 'rhs')), may hold values from -0.75 to 0.75
- near_blocks: bfloat16 [8192, 3, 128, 128], P('blk'), may hold values from -0.3125 to 0.3125
- near_list: int32 [8192, 3], P('blk'), may hold values from 0 to 8191, as said below
Outputs:
- applied: float32 [64, 1048576], P('rhs', 'blk')
Inputs may be any that keep to these rules, and one draw needn't show every extreme that they name: near_list[b, 0] = b, near_list[b, 1] is one or two boxes before b and near_list[b, 2] one or two boxes after b, counted around the closed boundary of 8192 boxes.
All inputs are finite; a program needn't handle non-finite values.
Results may differ from a plain program's by a relative error of at most 0.0029.
Values may be sent and summed in bfloat16 or wider, within the bound.
No kernel may reach another device: no remote copies, remote signals or barrier semaphores. Data moves between devices by JAX's collectives and lax.ppermute only.
A program may use at most 128 MiB of HBM per device.

v0:
```python
import jax
import jax.numpy as jnp
from jax import lax
from jax.experimental import pallas as pl
from jax.experimental.pallas import tpu as pltpu
from jax.sharding import PartitionSpec as P

RANK = 32
LEAF = 128
COLS = 32
F32 = jnp.float32
BF16 = jnp.bfloat16
NT = (((1,), (1,)), ((), ()))


def lane_block():
    return lax.broadcasted_iota(jnp.int32, (8, 128), 1) // RANK


def spread_factors(factors, rows):
    def run(first):
        block = lane_block()
        even = (block % 2) == 0
        left = block < 2
        for high in range(RANK // 4):
            pair0 = factors[pl.ds(first, 16), pl.ds(high * 128, 128)].astype(F32)
            pair1 = factors[pl.ds(first, 16), pl.ds(1024 + high * 128, 128)].astype(F32)
            for part in range(2):
                kid0 = pair0[part * 8 : part * 8 + 8]
                kid1 = pair1[part * 8 : part * 8 + 8]
                outer = jnp.where(even, kid0, pltpu.roll(kid1, 32, 1))
                inner = jnp.where(even, pltpu.roll(kid0, 96, 1), kid1)
                outer_swap = pltpu.roll(outer, 64, 1)
                inner_swap = pltpu.roll(inner, 64, 1)
                lines = (
                    jnp.where(left, outer, outer_swap),
                    jnp.where(left, inner, inner_swap),
                    jnp.where(left, outer_swap, outer),
                    jnp.where(left, inner_swap, inner),
                )
                for low in range(4):
                    start = (first + part * 8) * RANK + high * 4 + low
                    rows[pl.ds(start, 8, stride=RANK), :] = lines[low]

    return run


def split(value):
    high = value.astype(BF16)
    return high, (value - high.astype(F32)).astype(BF16)


def group_product(index, freqs, rows, high, low):
    kid0 = (2 * index - (index & (freqs - 1))) * RANK
    kid1 = kid0 + freqs * RANK
    kid0 = pl.multiple_of(kid0, RANK)
    kid1 = pl.multiple_of(kid1, RANK)
    left = rows[pl.ds(index * 2 * RANK, 2 * RANK), :].astype(BF16)
    right = jnp.concatenate(
        [
            high[pl.ds(kid0, RANK), :],
            high[pl.ds(kid1, RANK), :],
            low[pl.ds(kid0, RANK), :],
            low[pl.ds(kid1, RANK), :],
        ],
        axis=0,
    )
    return jnp.dot(left, right, preferred_element_type=F32)


def run_level(groups, freqs, factors, rows, source, target, finish=None):
    spread = spread_factors(factors, rows)
    for first in range(0, 2 * groups, 16):
        spread(first)
        for index in range(first // 2, first // 2 + 8):
            value = group_product(index, freqs, rows, source[0], source[1])
            if finish is None:
                top, rest = split(value)
                target[0][pl.ds(index * 2 * RANK, 2 * RANK), :] = top
                target[1][pl.ds(index * 2 * RANK, 2 * RANK), :] = rest
            else:
                finish(index, value)


LEAF_STEPS = 4


def outer_kernel(rhs, basis, factors, boxes_out, out, rows, high0, low0, high1, low1):
    step = pl.program_id(0)
    levels = pl.num_programs(0) - LEAF_STEPS
    level = step - LEAF_STEPS

    @pl.when(step < LEAF_STEPS)
    def _():
        count = basis.shape[0]
        base = step * count * RANK
        for box in range(count):
            piece = rhs[:, pl.ds(box * LEAF, LEAF)].astype(BF16)
            boxes_out[box] = piece
            value = lax.dot_general(basis[box], piece, NT, preferred_element_type=F32)
            top, rest = split(value)
            at = pl.multiple_of(base + box * RANK, RANK)
            high0[pl.ds(at, RANK), :] = top
            low0[pl.ds(at, RANK), :] = rest

    groups = high0.shape[0] // (2 * RANK)
    freqs = lax.shift_left(jnp.int32(1), jnp.maximum(level, 0))
    inside = (level >= 0) & (level < levels - 1)
    factor = factors.at[0]

    @pl.when(inside & (level % 2 == 0))
    def _():
        run_level(groups, freqs, factor, rows, (high0, low0), (high1, low1))

    @pl.when(inside & (level % 2 == 1))
    def _():
        run_level(groups, freqs, factor, rows, (high1, low1), (high0, low0))

    @pl.when(level == levels - 1)
    def _():
        def pack(index, value):
            parts = []
            for freq in range(2):
                lines = [
                    value[freq * RANK + 8 * part : freq * RANK + 8 * part + 8] for part in range(4)
                ]
                parts.append(jnp.concatenate(lines, axis=1))
            out[pl.ds(index * 16, 16), :] = jnp.concatenate(parts, axis=0).astype(BF16)

        run_level(groups, freqs, factor, rows, (high0, low0), None, pack)


def outer(rhs, basis, factors):
    boxes = basis.shape[0]
    levels = factors.shape[0]
    per = boxes // LEAF_STEPS
    last = LEAF_STEPS - 1
    state = pltpu.VMEM((boxes * RANK, COLS), BF16)
    return pl.pallas_call(
        outer_kernel,
        grid=(LEAF_STEPS + levels,),
        in_specs=[
            pl.BlockSpec((COLS, per * LEAF), lambda i: (0, jnp.minimum(i, last))),
            pl.BlockSpec((per, RANK, LEAF), lambda i: (jnp.minimum(i, last), 0, 0)),
            pl.BlockSpec(
                (1, boxes, 2 * RANK * RANK), lambda i: (jnp.maximum(i - LEAF_STEPS, 0), 0, 0)
            ),
        ],
        out_specs=[
            pl.BlockSpec((per, COLS, LEAF), lambda i: (jnp.minimum(i, last), 0, 0)),
            pl.BlockSpec((boxes * 8, 128), lambda i: (0, 0)),
        ],
        out_shape=[
            jax.ShapeDtypeStruct((boxes, COLS, LEAF), BF16),
            jax.ShapeDtypeStruct((boxes * 8, 128), BF16),
        ],
        scratch_shapes=[pltpu.VMEM((boxes * RANK, 128), F32), state, state, state, state],
        compiler_params=pltpu.CompilerParams(vmem_limit_bytes=56 * 2**20),
        cost_estimate=pl.CostEstimate(
            flops=4 * 10**8, bytes_accessed=8 * 10**6, transcendentals=0
        ),
        name="outer_levels",
    )(rhs, basis, factors)


def near_kernel(index, blocks, boxes, low, high, out, wide):
    step = pl.program_id(0)
    count = boxes.shape[0]
    per = blocks.shape[0]

    @pl.when(step == 0)
    def _():
        wide[pl.ds(2, count)] = boxes[...]
        for side in range(2):
            wide[side] = low[:, side * LEAF : (side + 1) * LEAF]
            wide[count + 2 + side] = high[:, side * LEAF : (side + 1) * LEAF]

    for box in range(per):
        total = None
        for side in range(3):
            piece = wide[index[(step * per + box) * 3 + side]]
            term = lax.dot_general(piece, blocks[box, side], NT, preferred_element_type=F32)
            total = term if total is None else total + term
        out[:, box * LEAF : (box + 1) * LEAF] = total


def near_field(index, blocks, boxes, low, high):
    count = blocks.shape[0]
    per = 8
    return pl.pallas_call(
        near_kernel,
        grid_spec=pltpu.PrefetchScalarGridSpec(
            num_scalar_prefetch=1,
            grid=(count // per,),
            in_specs=[
                pl.BlockSpec((per, 3, LEAF, LEAF), lambda i, s: (i, 0, 0, 0)),
                pl.BlockSpec((count, COLS, LEAF), lambda i, s: (0, 0, 0)),
                pl.BlockSpec((COLS, 2 * LEAF), lambda i, s: (0, 0)),
                pl.BlockSpec((COLS, 2 * LEAF), lambda i, s: (0, 0)),
            ],
            out_specs=pl.BlockSpec((COLS, per * LEAF), lambda i, s: (0, i)),
            scratch_shapes=[pltpu.VMEM((count + 4, COLS, LEAF), BF16)],
        ),
        out_shape=jax.ShapeDtypeStruct((COLS, count * LEAF), F32),
        compiler_params=pltpu.CompilerParams(vmem_limit_bytes=56 * 2**20),
        cost_estimate=pl.CostEstimate(
            flops=5 * 10**8, bytes_accessed=16 * 10**6, transcendentals=0
        ),
        name="near_field",
    )(index, blocks, boxes, low, high)


def inner_kernel(side, arrived, factors, own, sent, rows, high0, low0, high1, low1):
    level = pl.program_id(0)
    levels = pl.num_programs(0)
    sources = arrived.shape[0] // 16
    groups = sources // 2

    @pl.when(level == 0)
    def _():
        block = lane_block()
        for source in range(sources):
            both = arrived[pl.ds(source * 16, 16), :].astype(F32)
            first, second = both[:8], both[8:]
            parts = []
            for part in range(4):
                left = first if part == 0 else pltpu.roll(first, 128 - 32 * part, 1)
                right = second if part == 1 else pltpu.roll(second, (160 - 32 * part) % 128, 1)
                parts.append(jnp.where(block == 0, left, right)[:, : 2 * COLS])
            high0[pl.ds(source * RANK, RANK), :] = jnp.concatenate(parts, axis=0).astype(BF16)
        low0[...] = jnp.zeros_like(low0)

    freqs = lax.shift_left(jnp.int32(1), level)
    factor = factors.at[0]

    @pl.when((level < levels - 1) & (level % 2 == 0))
    def _():
        run_level(groups, freqs, factor, rows, (high0, low0), (high1, low1))

    @pl.when((level < levels - 1) & (level % 2 == 1))
    def _():
        run_level(groups, freqs, factor, rows, (high1, low1), (high0, low0))

    @pl.when(level == levels - 1)
    def _():
        kept = {}
        mine = side[0] == 0

        def pack(index, value):
            kept[index] = value
            if index % 2 == 0:
                return
            pieces = [
                kept[index - 1][:RANK],
                kept[index - 1][RANK:],
                kept[index][:RANK],
                kept[index][RANK:],
            ]
            first = jnp.concatenate([piece[:, :COLS] for piece in pieces], axis=1)
            second = jnp.concatenate([piece[:, COLS:] for piece in pieces], axis=1)
            own[index // 2] = jnp.where(mine, first, second).astype(BF16)
            sent[index // 2] = jnp.where(mine, second, first).astype(BF16)

        run_level(groups, freqs, factor, rows, (high1, low1), None, pack)


def inner(side, arrived, factors):
    levels, sources, width = factors.shape
    state = pltpu.VMEM((sources * RANK, 2 * COLS), BF16)
    packed = jax.ShapeDtypeStruct((sources // 4, RANK, 128), BF16)
    whole = pl.BlockSpec((sources // 4, RANK, 128), lambda i, s: (0, 0, 0))
    return pl.pallas_call(
        inner_kernel,
        grid_spec=pltpu.PrefetchScalarGridSpec(
            num_scalar_prefetch=1,
            grid=(levels,),
            in_specs=[
                pl.BlockSpec(arrived.shape, lambda i, s: (0, 0)),
                pl.BlockSpec((1, sources, width), lambda i, s: (i, 0, 0)),
            ],
            out_specs=[whole, whole],
            scratch_shapes=[pltpu.VMEM((sources * RANK, 128), F32), state, state, state, state],
        ),
        out_shape=[packed, packed],
        compiler_params=pltpu.CompilerParams(vmem_limit_bytes=56 * 2**20),
        cost_estimate=pl.CostEstimate(
            flops=2 * 10**8, bytes_accessed=2 * 10**6, transcendentals=0
        ),
        name="inner_levels",
    )(side, arrived, factors)


def expand_kernel(side, coeffs, expand, near, out):
    for quad in range(coeffs.shape[0]):
        turned = coeffs[quad].astype(F32).T.astype(BF16)
        for part in range(4):
            box = quad * 4 + part
            value = jnp.dot(
                turned[part * COLS : (part + 1) * COLS],
                expand[box],
                preferred_element_type=F32,
            )
            at = pl.ds(box * LEAF, LEAF)
            out[:, at] = near[:, at] + value


def expand_into(side, coeffs, expand, near):
    boxes = expand.shape[0]
    steps = 4
    per = boxes // steps
    return pl.pallas_call(
        expand_kernel,
        grid_spec=pltpu.PrefetchScalarGridSpec(
            num_scalar_prefetch=1,
            grid=(steps,),
            in_specs=[
                pl.BlockSpec((per // 4, RANK, 128), lambda i, s: (i, 0, 0)),
                pl.BlockSpec((per, RANK, LEAF), lambda i, s: (i, 0, 0)),
                pl.BlockSpec((COLS, per * LEAF), lambda i, s: (0, s[0] * steps + i)),
            ],
            out_specs=pl.BlockSpec((COLS, per * LEAF), lambda i, s: (0, s[0] * steps + i)),
        ),
        out_shape=jax.ShapeDtypeStruct(near.shape, F32),
        input_output_aliases={3: 0},
        compiler_params=pltpu.CompilerParams(vmem_limit_bytes=56 * 2**20),
        cost_estimate=pl.CostEstimate(
            flops=2 * 10**7, bytes_accessed=3 * 10**6, transcendentals=0
        ),
        name="expand_boxes",
    )(side, coeffs, expand, near)


def shards(
    rhs_vectors, leaf_basis, leaf_expand, outer_levels, inner_levels, near_blocks, near_list
):
    box_count = leaf_basis.shape[0]
    blocks = lax.axis_size("blk")
    swap = [(0, 1), (1, 0)]
    side = lax.axis_index("rhs").astype(jnp.int32).reshape(1)

    other_expand = lax.ppermute(leaf_expand, "rhs", swap)
    width = 2 * LEAF
    forward = [(i, (i + 1) % blocks) for i in range(blocks)]
    backward = [(i, (i - 1) % blocks) for i in range(blocks)]
    low = lax.ppermute(rhs_vectors[:, -width:].astype(BF16), "blk", forward)
    high = lax.ppermute(rhs_vectors[:, :width].astype(BF16), "blk", backward)

    total_boxes = box_count * blocks
    first_box = lax.axis_index("blk") * box_count
    local = jnp.arange(box_count, dtype=jnp.int32)
    offsets = jnp.mod(near_list - (first_box + local)[:, None] + total_boxes // 2, total_boxes)
    index = (local[:, None] + 2 + offsets - total_boxes // 2).reshape(-1)

    boxes, outgoing = outer(rhs_vectors, leaf_basis, outer_levels)
    outgoing, low, high, other_expand = lax.optimization_barrier(
        (outgoing, low, high, other_expand)
    )
    arrived = lax.all_to_all(outgoing, ("blk", "rhs"), split_axis=0, concat_axis=0, tiled=True)
    near = near_field(index, near_blocks, boxes, low, high)
    arrived, near = lax.optimization_barrier((arrived, near))
    own, sent = inner(side, arrived, inner_levels)
    other = lax.ppermute(sent, "rhs", swap)
    result = expand_into(side, own, leaf_expand, near)
    return expand_into(1 - side, other, other_expand, result)


def solution(mesh):
    in_specs = (
        P("rhs", "blk"),
        P("blk", None, None),
        P(("blk", "rhs"), None, None),
        P(None, "blk", None),
        P(None, ("blk", "rhs"), None),
        P("blk", None, None, None),
        P("blk", None),
    )
    out_specs = P("rhs", "blk")
    return jax.shard_map(shards, mesh=mesh, in_specs=in_specs, out_specs=out_specs, check_vma=False)
```

profile of v0, /device:TPU:1, one launch (start us, length us, event | category | flops | bytes accessed | tf_op | source)
XLA Modules:
  0.0 76.4 jit_solution(4798351303687978700)
XLA Ops:
  0.0 2.1 %collective-permute-start.2 = (bf16[64,32,128]{2,1,0:T(8,128)(2,1)}, bf16[64,32,128]{2,1,0:T(8,128)(2,1)S(1)}, u32[]{:S(2)}, u32[]{:S(2)}) collective-permute-start(bf16[64,32,128]{2,1,0:T(8,128)(2,1)} %expand.1), channel_id=1, source_target_pairs={{0,1},{1,0},{2,3},{3,2},{4,5},{5,4},{6,7},{7,6},{8,9},{9,8},{10,11... | collective-permute-start | bytes 1572872 | tf_op jit(solution)/shard_map/ppermute | solution.py:341
  2.1 1.7 %convert.4 = bf16[32,16384]{1,0:T(8,128)(2,1)S(1)} convert(f32[32,16384]{1,0:T(8,128)} %rhs.1) | non-fusion elementwise | flops 524288 | bytes 3145728 | tf_op jit(solution)/shard_map/convert.1
  3.8 2.5 %collective-permute-start = (bf16[32,256]{1,0:T(8,128)(2,1)S(1)}, bf16[32,256]{1,0:T(8,128)(2,1)S(1)}, u32[]{:S(2)}, u32[]{:S(2)}) collective-permute-start(bf16[32,256]{1,0:T(8,128)(2,1)S(1)} %get-tuple-element.26), channel_id=1, source_target_pairs={{0,2},{2,4},{4,6},{6,8},{8,10},{10,12},{12,14},{14,16},{16,18},{18... | collective-permute-start | bytes 49160 | tf_op jit(solution)/shard_map/ppermute | solution.py:345
  6.4 0.0 collective-permute-start.1
  6.4 0.0 copy-start.5
  6.4 22.0 %outer_levels.1 = (bf16[128,32,128]{2,1,0:T(8,128)(2,1)}, bf16[1024,128]{1,0:T(8,128)(2,1)}) custom-call(f32[32,16384]{1,0:T(8,128)} %rhs.1, bf16[128,32,128]{2,1,0:T(8,128)(2,1)} %basis.1, bf16[7,128,2048]{2,1,0:T(8,128)(2,1)} %factors.2), custom_call_target="tpu_custom_call" | custom-call | flops 400000000 | bytes 8000000 | tf_op jit(solution)/shard_map/outer_levels/pallas_call | solution.py:139
  28.4 0.0 collective-permute-done.low
  28.4 0.0 copy-start.3
  28.4 0.0 collective-permute-done.1.high
  28.4 0.0 copy-start.4
  28.4 0.0 collective-permute-done.2.expand
  28.4 0.0 copy-start.1
  28.4 10.1 %all-to-all-start = ((bf16[128,8,128]{2,1,0:T(8,128)(2,1)}), bf16[128,8,128]{2,1,0:T(8,128)(2,1)S(1)}, u32[]{:S(2)}, u32[]{:S(2)}) async-start(bf16[128,8,128]{2,1,0:T(8,128)(2,1)} %bitcast.4), calls=%async_computation | async-start | bytes 524288 | tf_op jit(solution)/shard_map/all_to_all | solution.py:358
  38.5 0.0 copy-done.5
  38.5 0.1 copy.10
  38.6 0.8 %reshape.18.index = s32[384]{0:T(512)} reshape(s32[128,3]{1,0:T(8,128)S(1)} %copy.10) | data formatting | bytes 3072 | tf_op jit(solution)/shard_map/reshape | solution.py:352
  39.4 0.0 copy-done.3
  39.4 0.0 copy-done.4
  39.4 16.4 %near_field.1.near = f32[32,16384]{1,0:T(8,128)} custom-call(s32[384]{0:T(512)} %reshape.18.index, bf16[128,3,128,128]{3,2,1,0:T(8,128)(2,1)} %blocks.1, bf16[128,32,128]{2,1,0:T(8,128)(2,1)} %get-tuple-element.17.boxes, bf16[32,256]{1,0:T(8,128)(2,1)} %copy-done.3, bf16[32,256]{1,0:T(8,128)(2,1)} %copy-done.4), custom_call_target="tpu_custom_call" | custom-call | flops 500000000 | bytes 16000000 | tf_op jit(solution)/shard_map/near_field/pallas_call | solution.py:190
  55.8 0.0 copy-done.1
  55.8 0.0 all-to-all-done
  55.8 0.0 copy-start
  55.8 0.7 copy-done
  56.5 9.8 %inner_levels.1 = (bf16[16,32,128]{2,1,0:T(8,128)(2,1)}, bf16[16,32,128]{2,1,0:T(8,128)(2,1)}) custom-call(s32[1]{0:T(128)} %bitcast.side, bf16[1024,128]{1,0:T(8,128)(2,1)} %bitcast.3, bf16[6,64,2048]{2,1,0:T(8,128)(2,1)} %factors.3), custom_call_target="tpu_custom_call" | custom-call | flops 200000000 | bytes 2000000 | tf_op jit(solution)/shard_map/inner_levels/pallas_call | solution.py:272
  66.3 1.4 %collective-permute-start.3 = (bf16[16,32,128]{2,1,0:T(8,128)(2,1)}, bf16[16,32,128]{2,1,0:T(8,128)(2,1)S(1)}, u32[]{:S(2)}, u32[]{:S(2)}) collective-permute-start(bf16[16,32,128]{2,1,0:T(8,128)(2,1)} %get-tuple-element.21), channel_id=1, source_target_pairs={{0,1},{1,0},{2,3},{3,2},{4,5},{5,4},{6,7},{7,6},{8,9},{9,8},{10,11... | collective-permute-start | bytes 393224 | tf_op jit(solution)/shard_map/ppermute | solution.py:362
  67.7 4.0 %expand_boxes.2.near = f32[32,16384]{1,0:T(8,128)} custom-call(s32[1]{0:T(128)} %bitcast.side, bf16[16,32,128]{2,1,0:T(8,128)(2,1)} %get-tuple-element.23.coeffs, bf16[64,32,128]{2,1,0:T(8,128)(2,1)} %expand.1, f32[32,16384]{1,0:T(8,128)} %near_field.1.near), custom_call_target="tpu_custom_call", output_to_operand_aliasing={{}: (3, {})} | custom-call | flops 20000000 | bytes 3000000 | tf_op jit(solution)/shard_map/expand_boxes/pallas_call | solution.py:311
  71.8 0.0 collective-permute-done.3.coeffs
  71.8 0.0 copy-start.2
  71.8 0.7 copy-done.2
  72.4 4.0 %expand_boxes.3 = f32[32,16384]{1,0:T(8,128)} custom-call(s32[1]{0:T(128)S(6)} %sub.14.side, bf16[16,32,128]{2,1,0:T(8,128)(2,1)} %copy-done.2, bf16[64,32,128]{2,1,0:T(8,128)(2,1)} %copy-done.1, f32[32,16384]{1,0:T(8,128)} %expand_boxes.2.near), custom_call_target="tpu_custom_call", output_to_operand_aliasing={{}: (3, {})} | custom-call | flops 20000000 | bytes 3000000 | tf_op jit(solution)/shard_map/expand_boxes/pallas_call | solution.py:311
  (3 shorter events, 0.0 us)
Async XLA Ops:
  0.0 28.4 %collective-permute-start.2 = (bf16[64,32,128]{2,1,0:T(8,128)(2,1)}, bf16[64,32,128]{2,1,0:T(8,128)(2,1)S(1)}, u32[]{:S(2)}, u32[]{:S(2)}) collective-permute-start(bf16[64,32,128]{2,1,0:T(8,128)(2,1)} %expand.1), channel_id=1, source_target_pairs={{0,1},{1,0},{2,3},{3,2},{4,5},{5,4},{6,7},{7,6},{8,9},{9,8},{10,11... | collective-permute-start | bytes 1572872 | tf_op jit(solution)/shard_map/ppermute | solution.py:341
  3.8 24.5 %collective-permute-start = (bf16[32,256]{1,0:T(8,128)(2,1)S(1)}, bf16[32,256]{1,0:T(8,128)(2,1)S(1)}, u32[]{:S(2)}, u32[]{:S(2)}) collective-permute-start(bf16[32,256]{1,0:T(8,128)(2,1)S(1)} %get-tuple-element.26), channel_id=1, source_target_pairs={{0,2},{2,4},{4,6},{6,8},{8,10},{10,12},{12,14},{14,16},{16,18},{18... | collective-permute-start | bytes 49160 | tf_op jit(solution)/shard_map/ppermute | solution.py:345
  6.4 22.0 %collective-permute-start.1 = (bf16[32,256]{1,0:T(8,128)(2,1)S(1)}, bf16[32,256]{1,0:T(8,128)(2,1)S(1)}, u32[]{:S(2)}, u32[]{:S(2)}) collective-permute-start(bf16[32,256]{1,0:T(8,128)(2,1)S(1)} %get-tuple-element.25), channel_id=1, source_target_pairs={{0,126},{2,0},{4,2},{6,4},{8,6},{10,8},{12,10},{14,12},{16,14},{18... | collective-permute-start | bytes 49160 | tf_op jit(solution)/shard_map/ppermute | solution.py:346
  6.4 32.1 %copy-start.5 = (s32[128,3]{0,1:T(4,128)S(1)}, s32[128,3]{0,1:T(4,128)}, u32[]{:S(2)}) copy-start(s32[128,3]{0,1:T(4,128)} %param.13) | copy-start | bytes 4612
  28.4 11.1 %copy-start.3 = (bf16[32,256]{1,0:T(8,128)(2,1)}, bf16[32,256]{1,0:T(8,128)(2,1)S(1)}, u32[]{:S(2)}) copy-start(bf16[32,256]{1,0:T(8,128)(2,1)S(1)} %collective-permute-done.low) | copy-start | bytes 49156
  28.4 11.0 %copy-start.4 = (bf16[32,256]{1,0:T(8,128)(2,1)}, bf16[32,256]{1,0:T(8,128)(2,1)S(1)}, u32[]{:S(2)}) copy-start(bf16[32,256]{1,0:T(8,128)(2,1)S(1)} %collective-permute-done.1.high) | copy-start | bytes 49156
  28.4 27.4 %copy-start.1 = (bf16[64,32,128]{2,1,0:T(8,128)(2,1)}, bf16[64,32,128]{2,1,0:T(8,128)(2,1)S(1)}, u32[]{:S(2)}) copy-start(bf16[64,32,128]{2,1,0:T(8,128)(2,1)S(1)} %collective-permute-done.2.expand) | copy-start | bytes 1572868
  28.4 27.4 %all-to-all-start = ((bf16[128,8,128]{2,1,0:T(8,128)(2,1)}), bf16[128,8,128]{2,1,0:T(8,128)(2,1)S(1)}, u32[]{:S(2)}, u32[]{:S(2)}) async-start(bf16[128,8,128]{2,1,0:T(8,128)(2,1)} %bitcast.4), calls=%async_computation | async-start | bytes 524288 | tf_op jit(solution)/shard_map/all_to_all | solution.py:358
  55.8 0.7 copy-start
  66.3 5.4 %collective-permute-start.3 = (bf16[16,32,128]{2,1,0:T(8,128)(2,1)}, bf16[16,32,128]{2,1,0:T(8,128)(2,1)S(1)}, u32[]{:S(2)}, u32[]{:S(2)}) collective-permute-start(bf16[16,32,128]{2,1,0:T(8,128)(2,1)} %get-tuple-element.21), channel_id=1, source_target_pairs={{0,1},{1,0},{2,3},{3,2},{4,5},{5,4},{6,7},{7,6},{8,9},{9,8},{10,11... | collective-permute-start | bytes 393224 | tf_op jit(solution)/shard_map/ppermute | solution.py:362
  71.8 0.7 copy-start.2
where the time goes:
time: 77.2 us; the launch traced here: 76.4 us
  Pallas kernels  56.2 us (73%)
  starting transfers between devices  16.1 us (21%)
  local copies, waits for them, and re-layouts  2.29 us (3%)
  other arithmetic  1.71 us (2%)
    pallas_call x1, Pallas kernels, outer(): pl.pallas_call(outer_kernel, grid=(LEAF_STEPS + levels,), in_specs=[pl.Bl...  22 us
    pallas_call x1, Pallas kernels, near_field(): pl.pallas_call(near_kernel, grid_spec=pltpu.PrefetchScalarGridSpec(num_sc...  16.4 us
    all_to_all x1, starting transfers between devices, shards(): lax.all_to_all(outgoing, ('blk', 'rhs'), split_axis=0, concat_axis=0, til...  10.1 us
    pallas_call x1, Pallas kernels, inner(): pl.pallas_call(inner_kernel, grid_spec=pltpu.PrefetchScalarGridSpec(num_s...  9.82 us
    pallas_call x2, Pallas kernels, expand_into(): pl.pallas_call(expand_kernel, grid_spec=pltpu.PrefetchScalarGridSpec(num_...  8.04 us
    ppermute x1, starting transfers between devices, shards(): low = lax.ppermute(rhs_vectors[:, -width:].astype(BF16), 'blk', forward)  2.55 us
    ppermute x1, starting transfers between devices, shards(): other_expand = lax.ppermute(leaf_expand, 'rhs', swap)  2.13 us
    another operation x1, other arithmetic  1.69 us
  transfers between devices with their start and end apart: 5, of which 0 were waited for; matrix products, arithmetic and copies ran while one was open for 3% of the time, Pallas kernels for 55%

commit v1 on v0

v1 whole, which is shorter than its diff:
```python
import jax
import jax.numpy as jnp
from jax import lax
from jax.experimental import pallas as pl
from jax.experimental.pallas import tpu as pltpu
from jax.sharding import PartitionSpec as P

RANK = 32
LEAF = 128
COLS = 32
F32 = jnp.float32
BF16 = jnp.bfloat16
NT = (((1,), (1,)), ((), ()))


NATURAL = (((0, 0), (1, 32), (2, 32), (3, 64)), ((4, 64), (5, 96), (6, 96), (7, 0)))
PAIRED = (((0, 0), (1, 32), (4, 0), (5, 32)), ((2, 96), (3, 0), (6, 96), (7, 0)))


def lane_block():
    return lax.broadcasted_iota(jnp.int32, (8, 128), 1) // RANK


def pick(choices):
    block = lane_block()
    low = jnp.where(block == 0, choices[0], choices[1])
    high = jnp.where(block == 2, choices[2], choices[3])
    return jnp.where(block < 2, low, high)


def factor_rows(factors, first):
    block = lax.broadcasted_iota(jnp.int32, (16, 128), 1) // RANK
    even = (block % 2) == 0
    left = block < 2
    rows = ([], [])
    for high in range(RANK // 4):
        kid0 = factors[pl.ds(first, 16), pl.ds(high * 128, 128)]
        kid1 = factors[pl.ds(first, 16), pl.ds(1024 + high * 128, 128)]
        outer = jnp.where(even, kid0, pltpu.roll(kid1, 32, 1))
        inner = jnp.where(even, pltpu.roll(kid0, 96, 1), kid1)
        outer_swap = pltpu.roll(outer, 64, 1)
        inner_swap = pltpu.roll(inner, 64, 1)
        for line in (
            jnp.where(left, outer, outer_swap),
            jnp.where(left, inner, inner_swap),
            jnp.where(left, outer_swap, outer),
            jnp.where(left, inner_swap, inner),
        ):
            wide = line.astype(F32)
            rows[0].append(wide[:8])
            rows[1].append(wide[8:])
    return [jnp.concatenate(part, axis=0).astype(BF16) for part in rows]


def split(value):
    high = value.astype(BF16)
    return high, (value - high.astype(F32)).astype(BF16)


def gathered(stage, layout):
    parts = []
    block = lane_block()
    shifts = sorted({shift for _, shift in layout})
    for part in range(4):
        total = None
        for shift in shifts:
            merged = None
            for lane, (freq, amount) in enumerate(layout):
                if amount != shift:
                    continue
                value = stage[pl.ds(part * 64 + freq, 8, stride=8), :]
                source = (lane - shift // 32) % 4
                merged = value if merged is None else jnp.where(block == source, value, merged)
            if shift:
                merged = pltpu.roll(merged, shift, 1)
            if total is None:
                total = merged
            else:
                mask = None
                for lane, (_, amount) in enumerate(layout):
                    if amount == shift:
                        here = block == lane
                        mask = here if mask is None else mask | here
                total = jnp.where(mask, merged, total)
        parts.append(total)
    return jnp.concatenate(parts, axis=0)


def put_state(state, at, value):
    high, low = split(value)
    state[0][at] = high
    state[1][at] = low


def run_level(step, layouts, factors, source, target, stage):
    sets = source[0].shape[0]
    blocks = source[0].shape[1] // 2
    for first in range(0, 8 * blocks, 16):
        both = factor_rows(factors, first)
        for part in range(2):
            m = first // 8 + part
            near = 2 * m - (m & (step - 1))
            far = near + step
            for which in range(sets):
                right = jnp.concatenate(
                    [
                        source[0][which, near],
                        source[0][which, far],
                        source[1][which, near],
                        source[1][which, far],
                    ],
                    axis=0,
                )
                slot = stage.at[m * sets + which]
                slot[...] = jnp.dot(both[part], right, preferred_element_type=F32)
                for half, layout in enumerate(layouts):
                    put_state(target, (which, 2 * m + half), gathered(slot, layout))


def level_step(level):
    return jnp.maximum(lax.shift_left(jnp.int32(1), jnp.maximum(level - 2, 0)), 1)


LEAF_STEPS = 4


def outer_kernel(
    rhs_hbm, basis_hbm, factors_hbm, boxes_out, out, rhs, basis, factors, stage, high0, low0, high1, low1, sems
):
    levels = factors.shape[0]
    count = basis.shape[0]
    per = count // LEAF_STEPS

    def leaf_copies(step):
        columns = pl.ds(pl.multiple_of(step * per * LEAF, LEAF), per * LEAF)
        boxes = pl.ds(step * per, per)
        return (
            pltpu.make_async_copy(rhs_hbm.at[:, columns], rhs.at[:, columns], sems.at[0, step]),
            pltpu.make_async_copy(basis_hbm.at[boxes], basis.at[boxes], sems.at[1, step]),
        )

    def level_copy(level):
        return pltpu.make_async_copy(factors_hbm.at[level], factors.at[level], sems.at[2, level])

    for step in range(LEAF_STEPS):
        for copy in leaf_copies(step):
            copy.start()
    for level in range(levels):
        level_copy(level).start()

    def leaf(step, carry):
        for copy in leaf_copies(step):
            copy.wait()
        for group in range(per // 8):
            first = step * per + group * 8
            at = pl.ds(pl.multiple_of(first * LEAF, LEAF), 8 * LEAF)
            columns = rhs[:, at].astype(BF16)
            pieces = [columns[:, box * LEAF : (box + 1) * LEAF] for box in range(8)]
            for box in range(8):
                boxes_out[first + box] = pieces[box]
            for kid in range(2):
                left = jnp.concatenate([basis[first + kid + 2 * i] for i in range(4)], axis=0)
                right = jnp.concatenate([pieces[kid + 2 * i] for i in range(4)], axis=0)
                value = lax.dot_general(left, right, NT, preferred_element_type=F32)
                parts = []
                for part in range(4):
                    at = [i * RANK + part * 8 for i in range(4)]
                    parts.append(pick([value[i : i + 8] for i in at]))
                at = step * (per // 4) + 2 * group + kid
                put_state((high0, low0), (0, at), jnp.concatenate(parts, axis=0))
        return carry

    lax.fori_loop(0, LEAF_STEPS, leaf, 0)

    even, odd = (high0, low0), (high1, low1)
    level_copy(0).wait()
    run_level(1, PAIRED, factors.at[0], even, odd, stage)

    def two_levels(pair, carry):
        level = 2 * pair + 1
        level_copy(level).wait()
        run_level(level_step(level), NATURAL, factors.at[level], odd, even, stage)
        level_copy(level + 1).wait()
        run_level(level_step(level + 1), NATURAL, factors.at[level + 1], even, odd, stage)
        return carry

    lax.fori_loop(0, (levels - 1) // 2, two_levels, 0)

    for block in range(count // 4):
        value = high1[0, block].astype(F32)
        for pair in range(2):
            parts = []
            for freq in (2 * pair, 2 * pair + 1):
                lines = []
                for part in range(4):
                    shift = (part - freq) * 32 % 128
                    line = value[part * 8 : part * 8 + 8]
                    lines.append(pltpu.roll(line, shift, 1) if shift else line)
                parts.append(pick(lines))
            at = pl.ds((2 * block + pair) * 16, 16)
            out[at, :] = jnp.concatenate(parts, axis=0).astype(BF16)


def outer(rhs, basis, factors):
    boxes = basis.shape[0]
    levels = factors.shape[0]
    state = pltpu.VMEM((1, boxes // 4, RANK, 128), BF16)
    whole = pl.BlockSpec(memory_space=pl.ANY)
    return pl.pallas_call(
        outer_kernel,
        in_specs=[whole, whole, whole],
        out_specs=[pl.BlockSpec(memory_space=pltpu.VMEM), pl.BlockSpec(memory_space=pltpu.VMEM)],
        out_shape=[
            jax.ShapeDtypeStruct((boxes, COLS, LEAF), BF16),
            jax.ShapeDtypeStruct((boxes * 8, 128), BF16),
        ],
        scratch_shapes=[
            pltpu.VMEM(rhs.shape, F32),
            pltpu.VMEM(basis.shape, BF16),
            pltpu.VMEM(factors.shape, BF16),
            pltpu.VMEM((boxes // 8, 256, 128), F32),
            state,
            state,
            state,
            state,
            pltpu.SemaphoreType.DMA((3, max(LEAF_STEPS, levels))),
        ],
        compiler_params=pltpu.CompilerParams(vmem_limit_bytes=56 * 2**20),
        cost_estimate=pl.CostEstimate(
            flops=4 * 10**8, bytes_accessed=8 * 10**6, transcendentals=0
        ),
        name="outer_levels",
    )(rhs, basis, factors)


def near_kernel(index, blocks, boxes, low, high, out, wide):
    step = pl.program_id(0)
    count = boxes.shape[0]
    per = blocks.shape[0]

    @pl.when(step == 0)
    def _():
        wide[pl.ds(2, count)] = boxes[...]
        for side in range(2):
            wide[side] = low[:, side * LEAF : (side + 1) * LEAF].astype(BF16)
            wide[count + 2 + side] = high[:, side * LEAF : (side + 1) * LEAF].astype(BF16)

    for box in range(per):
        pieces = [wide[index[(step * per + box) * 3 + side]] for side in range(3)]
        left = jnp.concatenate(pieces, axis=1)
        right = jnp.concatenate([blocks[box, side] for side in range(3)], axis=1)
        out[:, box * LEAF : (box + 1) * LEAF] = lax.dot_general(
            left, right, NT, preferred_element_type=F32
        )


def near_field(index, blocks, boxes, low, high):
    count = blocks.shape[0]
    per = 8
    return pl.pallas_call(
        near_kernel,
        grid_spec=pltpu.PrefetchScalarGridSpec(
            num_scalar_prefetch=1,
            grid=(count // per,),
            in_specs=[
                pl.BlockSpec((per, 3, LEAF, LEAF), lambda i, s: (i, 0, 0, 0)),
                pl.BlockSpec((count, COLS, LEAF), lambda i, s: (0, 0, 0)),
                pl.BlockSpec((COLS, 2 * LEAF), lambda i, s: (0, 0)),
                pl.BlockSpec((COLS, 2 * LEAF), lambda i, s: (0, 0)),
            ],
            out_specs=pl.BlockSpec((COLS, per * LEAF), lambda i, s: (0, i)),
            scratch_shapes=[pltpu.VMEM((count + 4, COLS, LEAF), BF16)],
        ),
        out_shape=jax.ShapeDtypeStruct((COLS, count * LEAF), F32),
        compiler_params=pltpu.CompilerParams(vmem_limit_bytes=56 * 2**20),
        cost_estimate=pl.CostEstimate(
            flops=5 * 10**8, bytes_accessed=16 * 10**6, transcendentals=0
        ),
        name="near_field",
    )(index, blocks, boxes, low, high)


def inner_kernel(side, arrived, factors_hbm, out, factors, stage, high0, low0, high1, low1, sems):
    levels = factors.shape[0]
    sources = arrived.shape[0] // 16

    def level_copy(level):
        return pltpu.make_async_copy(factors_hbm.at[level], factors.at[level], sems.at[level])

    for level in range(levels):
        level_copy(level).start()

    low0[...] = jnp.zeros_like(low0)
    for first in range(0, sources, 8):
        both = [arrived[pl.ds((first + i) * 16, 16), :].astype(F32) for i in range(8)]
        for which in range(2):
            sent = [value[which * 8 : which * 8 + 8] for value in both]
            for kid in range(2):
                parts = []
                for part in range(4):
                    lines = []
                    for i in range(4):
                        shift = (i - part) * 32 % 128
                        value = sent[kid + 2 * i]
                        lines.append(pltpu.roll(value, shift, 1) if shift else value)
                    parts.append(pick(lines))
                high0[which, first // 4 + kid] = jnp.concatenate(parts, axis=0).astype(BF16)

    even, odd = (high0, low0), (high1, low1)
    level_copy(0).wait()
    run_level(1, PAIRED, factors.at[0], even, odd, stage)

    def two_levels(pair, carry):
        level = 2 * pair + 1
        level_copy(level).wait()
        run_level(level_step(level), NATURAL, factors.at[level], odd, even, stage)
        level_copy(level + 1).wait()
        run_level(level_step(level + 1), NATURAL, factors.at[level + 1], even, odd, stage)
        return carry

    lax.fori_loop(0, (levels - 2) // 2, two_levels, 0)
    level_copy(levels - 1).wait()
    last = factors.at[levels - 1]
    run_level(level_step(levels - 1), NATURAL, last, odd, even, stage)
    for which in range(2):
        out[which ^ side[0]] = high0[which]


def inner(side, arrived, factors):
    levels, sources, _ = factors.shape
    state = pltpu.VMEM((2, sources // 4, RANK, 128), BF16)
    return pl.pallas_call(
        inner_kernel,
        in_specs=[
            pl.BlockSpec(memory_space=pltpu.SMEM),
            pl.BlockSpec(memory_space=pltpu.VMEM),
            pl.BlockSpec(memory_space=pl.ANY),
        ],
        out_specs=pl.BlockSpec(memory_space=pltpu.VMEM),
        out_shape=jax.ShapeDtypeStruct((2, sources // 4, RANK, 128), BF16),
        scratch_shapes=[
            pltpu.VMEM(factors.shape, BF16),
            pltpu.VMEM((sources // 4, 256, 128), F32),
            state,
            state,
            state,
            state,
            pltpu.SemaphoreType.DMA((levels,)),
        ],
        compiler_params=pltpu.CompilerParams(vmem_limit_bytes=56 * 2**20),
        cost_estimate=pl.CostEstimate(
            flops=2 * 10**8, bytes_accessed=2 * 10**6, transcendentals=0
        ),
        name="inner_levels",
    )(side, arrived, factors)


def expand_kernel(side, coeffs, expand, near, out):
    for quad in range(coeffs.shape[0]):
        turned = coeffs[quad].astype(F32).T.astype(BF16)
        for part in range(4):
            box = quad * 4 + part
            value = jnp.dot(
                turned[part * COLS : (part + 1) * COLS],
                expand[box],
                preferred_element_type=F32,
            )
            at = pl.ds(box * LEAF, LEAF)
            out[:, at] = near[:, at] + value


def expand_into(side, coeffs, expand, near):
    boxes = expand.shape[0]
    steps = 4
    per = boxes // steps
    return pl.pallas_call(
        expand_kernel,
        grid_spec=pltpu.PrefetchScalarGridSpec(
            num_scalar_prefetch=1,
            grid=(steps,),
            in_specs=[
                pl.BlockSpec((per // 4, RANK, 128), lambda i, s: (i, 0, 0)),
                pl.BlockSpec((per, RANK, LEAF), lambda i, s: (i, 0, 0)),
                pl.BlockSpec((COLS, per * LEAF), lambda i, s: (0, s[0] * steps + i)),
            ],
            out_specs=pl.BlockSpec((COLS, per * LEAF), lambda i, s: (0, s[0] * steps + i)),
        ),
        out_shape=jax.ShapeDtypeStruct(near.shape, F32),
        input_output_aliases={3: 0},
        compiler_params=pltpu.CompilerParams(vmem_limit_bytes=8 * 2**20),
        cost_estimate=pl.CostEstimate(
            flops=2 * 10**7, bytes_accessed=3 * 10**6, transcendentals=0
        ),
        name="expand_boxes",
    )(side, coeffs, expand, near)


def shards(
    rhs_vectors, leaf_basis, leaf_expand, outer_levels, inner_levels, near_blocks, near_list
):
    box_count = leaf_basis.shape[0]
    blocks = lax.axis_size("blk")
    swap = [(0, 1), (1, 0)]
    side = lax.axis_index("rhs").astype(jnp.int32).reshape(1)

    width = 2 * LEAF
    forward = [(i, (i + 1) % blocks) for i in range(blocks)]
    backward = [(i, (i - 1) % blocks) for i in range(blocks)]
    low = lax.ppermute(rhs_vectors[:, -width:], "blk", forward)
    high = lax.ppermute(rhs_vectors[:, :width], "blk", backward)

    total_boxes = box_count * blocks
    first_box = lax.axis_index("blk") * box_count
    local = jnp.arange(box_count, dtype=jnp.int32)
    offsets = jnp.mod(near_list - (first_box + local)[:, None] + total_boxes // 2, total_boxes)
    index = (local[:, None] + 2 + offsets - total_boxes // 2).reshape(-1)

    boxes, outgoing = outer(rhs_vectors, leaf_basis, outer_levels)
    outgoing, low, high, own_expand = lax.optimization_barrier((outgoing, low, high, leaf_expand))
    other_expand = lax.ppermute(own_expand, "rhs", swap)
    arrived = lax.all_to_all(outgoing, ("blk", "rhs"), split_axis=0, concat_axis=0, tiled=True)
    near = near_field(index, near_blocks, boxes, low, high)
    arrived, near = lax.optimization_barrier((arrived, near))
    coeffs = inner(side, arrived, inner_levels)
    other = lax.ppermute(coeffs[1], "rhs", swap)
    result = expand_into(side, coeffs[0], leaf_expand, near)
    return expand_into(1 - side, other, other_expand, result)


def solution(mesh):
    in_specs = (
        P("rhs", "blk"),
        P("blk", None, None),
        P(("blk", "rhs"), None, None),
        P(None, "blk", None),
        P(None, ("blk", "rhs"), None),
        P("blk", None, None, None),
        P("blk", None),
    )
    out_specs = P("rhs", "blk")
    return jax.shard_map(shards, mesh=mesh, in_specs=in_specs, out_specs=out_specs, check_vma=False)
```

time: 77.2 us -> 59.8 us (0.77)
  Pallas kernels: 56.2 us -> 39.9 us
  other arithmetic: 1.71 us -> 0.02 us
  starting transfers between devices: 16.1 us -> 15 us
  local copies, waits for them, and re-layouts: 2.29 us -> 3.39 us
    pallas_call x2, Pallas kernels: 31.8 us -> 16.9 us  [the longest x1 9.27 us: outer(): pl.pallas_call(outer_kernel, in_specs=[whole, whole, whole], out_specs=[p...]
    another operation x1 -> x0, other arithmetic: 1.69 us -> none
    ppermute x4, starting transfers between devices: 6.06 us -> 4.66 us  [the longest x1 3.03 us: shards(): low = lax.ppermute(rhs_vectors[:, -width:], 'blk', forward)]
    pallas_call x1, Pallas kernels: 16.4 us -> 15.4 us  [near_field(): pl.pallas_call(near_kernel, grid_spec=pltpu.PrefetchScalarGridSpec(num_sc...]
    squeeze x0 -> x1, local copies, waits for them, and re-layouts: none -> 0.99 us  [shards(): result = expand_into(side, coeffs[0], leaf_expand, near)]
    slice x1, local copies, waits for them, and re-layouts: 0.01 us -> 0.78 us  [shards(): high = lax.ppermute(rhs_vectors[:, :width], 'blk', backward)]
  transfers between devices with their start and end apart: 5 -> 5, of which waited for: 0 -> 1; matrix products, arithmetic and copies ran while one was open for 3% -> 3% of each run, Pallas kernels for 55% -> 61%
where the time goes in v1:
time: 59.8 us; the launch traced here: 58.9 us
  Pallas kernels  39.9 us (67%)
  starting transfers between devices  15 us (25%)
  local copies, waits for them, and re-layouts  3.39 us (6%)
    pallas_call x1, Pallas kernels, near_field(): pl.pallas_call(near_kernel, grid_spec=pltpu.PrefetchScalarGridSpec(num_sc...  15.4 us
    all_to_all x1, starting transfers between devices, shards(): lax.all_to_all(outgoing, ('blk', 'rhs'), split_axis=0, concat_axis=0, til...  10.3 us
    pallas_call x1, Pallas kernels, outer(): pl.pallas_call(outer_kernel, in_specs=[whole, whole, whole], out_specs=[p...  9.27 us
    pallas_call x2, Pallas kernels, expand_into(): pl.pallas_call(expand_kernel, grid_spec=pltpu.PrefetchScalarGridSpec(num_...  7.66 us
    pallas_call x1, Pallas kernels, inner(): pl.pallas_call(inner_kernel, in_specs=[pl.BlockSpec(memory_space=pltpu.SM...  7.63 us
    ppermute x1, starting transfers between devices, shards(): low = lax.ppermute(rhs_vectors[:, -width:], 'blk', forward)  3.03 us
    ppermute x1, starting transfers between devices, shards(): other_expand = lax.ppermute(own_expand, 'rhs', swap)  1.47 us
  transfers between devices with their start and end apart: 5, of which 1 were waited for; matrix products, arithmetic and copies ran while one was open for 3% of the time, Pallas kernels for 61%

profile of v1, /device:TPU:1, one launch (start us, length us, event | category | flops | bytes accessed | tf_op | source)
XLA Modules:
  0.0 58.9 jit_solution(18061467818831020852)
XLA Ops:
  0.0 0.8 %fusion.3 = (f32[32,256]{1,0:T(8,128)S(1)}, f32[32,256]{1,0:T(8,128)S(1)}) fusion(f32[32,16384]{1,0:T(8,128)} %rhs_hbm.1), kind=kLoop, calls=%fused_computation.10 | loop fusion | bytes 131072 | tf_op jit(solution)/shard_map/slice | solution.py:410
  0.8 3.0 %collective-permute-start = (f32[32,256]{1,0:T(8,128)S(1)}, f32[32,256]{1,0:T(8,128)S(1)}, u32[]{:S(2)}, u32[]{:S(2)}) collective-permute-start(f32[32,256]{1,0:T(8,128)S(1)} %get-tuple-element.22), channel_id=1, source_target_pairs={{0,2},{2,4},{4,6},{6,8},{8,10},{10,12},{12,14},{14,16},{16,18},{18... | collective-permute-start | bytes 98312 | tf_op jit(solution)/shard_map/ppermute | solution.py:409
  3.8 0.0 collective-permute-start.1
  3.8 0.0 copy-start
  3.8 0.0 copy-start.4
  3.8 9.3 %outer_levels.1 = (bf16[128,32,128]{2,1,0:T(8,128)(2,1)}, bf16[1024,128]{1,0:T(8,128)(2,1)}) custom-call(f32[32,16384]{1,0:T(8,128)} %rhs_hbm.1, bf16[128,32,128]{2,1,0:T(8,128)(2,1)} %basis_hbm.1, bf16[7,128,2048]{2,1,0:T(8,128)(2,1)} %factors_hbm.2), custom_call_target="tpu_custom_call" | custom-call | flops 400000000 | bytes 8000000 | tf_op jit(solution)/shard_map/outer_levels/pallas_call | solution.py:209
  13.1 0.0 collective-permute-done.low
  13.1 0.0 copy-start.2
  13.1 0.0 collective-permute-done.1.high
  13.1 0.0 copy-start.3
  13.1 10.3 %all-to-all-start = ((bf16[128,8,128]{2,1,0:T(8,128)(2,1)}), bf16[128,8,128]{2,1,0:T(8,128)(2,1)S(1)}, u32[]{:S(2)}, u32[]{:S(2)}) async-start(bf16[128,8,128]{2,1,0:T(8,128)(2,1)} %bitcast.8), calls=%async_computation | async-start | bytes 524288 | tf_op jit(solution)/shard_map/all_to_all | solution.py:421
  23.5 0.0 copy-done
  23.5 1.5 %collective-permute-start.3 = (bf16[64,32,128]{2,1,0:T(8,128)(2,1)S(1)}, bf16[64,32,128]{2,1,0:T(8,128)(2,1)S(1)}, u32[]{:S(2)}, u32[]{:S(2)}) collective-permute-start(bf16[64,32,128]{2,1,0:T(8,128)(2,1)S(1)} %copy-done), channel_id=1, source_target_pairs={{0,1},{1,0},{2,3},{3,2},{4,5},{5,4},{6,7},{7,6},{8,9},{9,8},{10,11... | collective-permute-start | bytes 1572872 | tf_op jit(solution)/shard_map/ppermute | solution.py:420
  25.0 0.0 copy-done.4
  25.0 0.1 copy.10
  25.1 0.8 %reshape.18.index = s32[384]{0:T(512)} reshape(s32[128,3]{1,0:T(8,128)S(1)} %copy.10) | data formatting | bytes 3072 | tf_op jit(solution)/shard_map/reshape | solution.py:416
  25.9 0.0 copy-done.2
  25.9 0.0 copy-done.3
  25.9 15.4 %near_field.1.near = f32[32,16384]{1,0:T(8,128)} custom-call(s32[384]{0:T(512)} %reshape.18.index, bf16[128,3,128,128]{3,2,1,0:T(8,128)(2,1)} %blocks.1, bf16[128,32,128]{2,1,0:T(8,128)(2,1)} %get-tuple-element.15.boxes, f32[32,256]{1,0:T(8,128)} %copy-done.2, f32[32,256]{1,0:T(8,128)} %copy-done.3), custom_call_target="tpu_custom_call" | custom-call | flops 500000000 | bytes 16000000 | tf_op jit(solution)/shard_map/near_field/pallas_call | solution.py:260
  41.3 0.0 all-to-all-done
  41.3 0.0 copy-start.1
  41.3 0.7 %copy-done.1 = bf16[128,8,128]{2,1,0:T(8,128)(2,1)} copy-done((bf16[128,8,128]{2,1,0:T(8,128)(2,1)}, bf16[128,8,128]{2,1,0:T(8,128)(2,1)S(1)}, u32[]{:S(2)}) %copy-start.1) | copy-done | bytes 262168
  42.0 7.6 %inner_levels.1 = bf16[2,16,32,128]{3,2,1,0:T(8,128)(2,1)} custom-call(s32[1]{0:T(128)} %bitcast.side, bf16[1024,128]{1,0:T(8,128)(2,1)} %bitcast.7, bf16[6,64,2048]{2,1,0:T(8,128)(2,1)} %factors_hbm.3), custom_call_target="tpu_custom_call" | custom-call | flops 200000000 | bytes 2000000 | tf_op jit(solution)/shard_map/inner_levels/pallas_call | solution.py:332
  49.6 1.0 %slice_bitcast_fusion = (bf16[16,32,128]{2,1,0:T(8,128)(2,1)S(1)}, bf16[16,32,128]{2,1,0:T(8,128)(2,1)S(1)}) fusion(bf16[2,16,32,128]{3,2,1,0:T(8,128)(2,1)} %inner_levels.1), kind=kLoop, calls=%fused_computation | loop fusion | bytes 524288 | tf_op jit(solution)/shard_map/squeeze | solution.py:426
  50.6 0.2 collective-permute-start.2
  50.8 3.8 %expand_boxes.2.near = f32[32,16384]{1,0:T(8,128)} custom-call(s32[1]{0:T(128)} %bitcast.side, bf16[16,32,128]{2,1,0:T(8,128)(2,1)S(1)} %get-tuple-element.23.coeffs, bf16[64,32,128]{2,1,0:T(8,128)(2,1)S(1)} %copy-done, f32[32,16384]{1,0:T(8,128)} %near_field.1.near), custom_call_target="tpu_custom_call", output_to_operand_aliasing={{}: (3, {})} | custom-call | flops 20000000 | bytes 3000000 | tf_op jit(solution)/shard_map/expand_boxes/pallas_call | solution.py:376
  54.6 0.5 collective-permute-done.2.coeffs
  55.1 0.0 collective-permute-done.3.expand
  55.1 3.8 %expand_boxes.3 = f32[32,16384]{1,0:T(8,128)} custom-call(s32[1]{0:T(128)S(6)} %sub.14.side, bf16[16,32,128]{2,1,0:T(8,128)(2,1)S(1)} %collective-permute-done.2.coeffs, bf16[64,32,128]{2,1,0:T(8,128)(2,1)S(1)} %collective-permute-done.3.expand, f32[32,16384]{1,0:T(8,128)} %expand_boxes.2.near), custom_call_target="tpu_custom_call", output_to_operand_aliasing={{}: (3, {})} | custom-call | flops 20000000 | bytes 3000000 | tf_op jit(solution)/shard_map/expand_boxes/pallas_call | solution.py:376
  (2 shorter events, 0.0 us)
Async XLA Ops:
  0.8 12.3 %collective-permute-start = (f32[32,256]{1,0:T(8,128)S(1)}, f32[32,256]{1,0:T(8,128)S(1)}, u32[]{:S(2)}, u32[]{:S(2)}) collective-permute-start(f32[32,256]{1,0:T(8,128)S(1)} %get-tuple-element.22), channel_id=1, source_target_pairs={{0,2},{2,4},{4,6},{6,8},{8,10},{10,12},{12,14},{14,16},{16,18},{18... | collective-permute-start | bytes 98312 | tf_op jit(solution)/shard_map/ppermute | solution.py:409
  3.8 9.3 %collective-permute-start.1 = (f32[32,256]{1,0:T(8,128)S(1)}, f32[32,256]{1,0:T(8,128)S(1)}, u32[]{:S(2)}, u32[]{:S(2)}) collective-permute-start(f32[32,256]{1,0:T(8,128)S(1)} %get-tuple-element.21), channel_id=1, source_target_pairs={{0,126},{2,0},{4,2},{6,4},{8,6},{10,8},{12,10},{14,12},{16,14},{18... | collective-permute-start | bytes 98312 | tf_op jit(solution)/shard_map/ppermute | solution.py:410
  3.8 19.7 %copy-start = (bf16[64,32,128]{2,1,0:T(8,128)(2,1)S(1)}, bf16[64,32,128]{2,1,0:T(8,128)(2,1)}, u32[]{:S(2)}) copy-start(bf16[64,32,128]{2,1,0:T(8,128)(2,1)} %expand.1) | copy-start | bytes 1572868
  3.8 21.2 %copy-start.4 = (s32[128,3]{0,1:T(4,128)S(1)}, s32[128,3]{0,1:T(4,128)}, u32[]{:S(2)}) copy-start(s32[128,3]{0,1:T(4,128)} %param.13) | copy-start | bytes 4612
  13.1 12.8 %copy-start.2 = (f32[32,256]{1,0:T(8,128)}, f32[32,256]{1,0:T(8,128)S(1)}, u32[]{:S(2)}) copy-start(f32[32,256]{1,0:T(8,128)S(1)} %collective-permute-done.low) | copy-start | bytes 98308
  13.1 12.8 %copy-start.3 = (f32[32,256]{1,0:T(8,128)}, f32[32,256]{1,0:T(8,128)S(1)}, u32[]{:S(2)}) copy-start(f32[32,256]{1,0:T(8,128)S(1)} %collective-permute-done.1.high) | copy-start | bytes 98308
  13.1 28.1 %all-to-all-start = ((bf16[128,8,128]{2,1,0:T(8,128)(2,1)}), bf16[128,8,128]{2,1,0:T(8,128)(2,1)S(1)}, u32[]{:S(2)}, u32[]{:S(2)}) async-start(bf16[128,8,128]{2,1,0:T(8,128)(2,1)} %bitcast.8), calls=%async_computation | async-start | bytes 524288 | tf_op jit(solution)/shard_map/all_to_all | solution.py:421
  23.5 31.6 %collective-permute-start.3 = (bf16[64,32,128]{2,1,0:T(8,128)(2,1)S(1)}, bf16[64,32,128]{2,1,0:T(8,128)(2,1)S(1)}, u32[]{:S(2)}, u32[]{:S(2)}) collective-permute-start(bf16[64,32,128]{2,1,0:T(8,128)(2,1)S(1)} %copy-done), channel_id=1, source_target_pairs={{0,1},{1,0},{2,3},{3,2},{4,5},{5,4},{6,7},{7,6},{8,9},{9,8},{10,11... | collective-permute-start | bytes 1572872 | tf_op jit(solution)/shard_map/ppermute | solution.py:420
  41.3 0.7 %copy-start.1 = (bf16[128,8,128]{2,1,0:T(8,128)(2,1)}, bf16[128,8,128]{2,1,0:T(8,128)(2,1)S(1)}, u32[]{:S(2)}) copy-start(bf16[128,8,128]{2,1,0:T(8,128)(2,1)S(1)} %all-to-all-done) | copy-start | bytes 786436
  50.6 4.5 %collective-permute-start.2 = (bf16[16,32,128]{2,1,0:T(8,128)(2,1)S(1)}, bf16[16,32,128]{2,1,0:T(8,128)(2,1)S(1)}, u32[]{:S(2)}, u32[]{:S(2)}) collective-permute-start(bf16[16,32,128]{2,1,0:T(8,128)(2,1)S(1)} %get-tuple-element.24), channel_id=1, source_target_pairs={{0,1},{1,0},{2,3},{3,2},{4,5},{5,4},{6,7},{7,6},{8,9},{9,8},{10,11... | collective-permute-start | bytes 393224 | tf_op jit(solution)/shard_map/ppermute | solution.py:425

commit v2 on v1

--- a/solution.py
+++ b/solution.py
@@ -233,45 +233,59 @@
     )(rhs, basis, factors)
 
 
-def near_kernel(index, blocks, boxes, low, high, out, wide):
-    step = pl.program_id(0)
+NEAR_STEPS = 16
+
+
+def near_kernel(index, blocks_hbm, boxes, low, high, out_hbm, wide, blocks, total, sems):
     count = boxes.shape[0]
-    per = blocks.shape[0]
-
-    @pl.when(step == 0)
-    def _():
-        wide[pl.ds(2, count)] = boxes[...]
-        for side in range(2):
-            wide[side] = low[:, side * LEAF : (side + 1) * LEAF].astype(BF16)
-            wide[count + 2 + side] = high[:, side * LEAF : (side + 1) * LEAF].astype(BF16)
-
-    for box in range(per):
-        pieces = [wide[index[(step * per + box) * 3 + side]] for side in range(3)]
-        left = jnp.concatenate(pieces, axis=1)
-        right = jnp.concatenate([blocks[box, side] for side in range(3)], axis=1)
-        out[:, box * LEAF : (box + 1) * LEAF] = lax.dot_general(
-            left, right, NT, preferred_element_type=F32
-        )
+    per = count // NEAR_STEPS
+
+    def load(step):
+        at = pl.ds(step * per, per)
+        return pltpu.make_async_copy(blocks_hbm.at[at], blocks.at[at], sems.at[0, step])
+
+    def store(step):
+        at = pl.ds(pl.multiple_of(step * per * LEAF, LEAF), per * LEAF)
+        return pltpu.make_async_copy(total.at[:, at], out_hbm.at[:, at], sems.at[1, step])
+
+    for step in range(NEAR_STEPS):
+        load(step).start()
+    wide[pl.ds(2, count)] = boxes[...]
+    for side in range(2):
+        wide[side] = low[:, side * LEAF : (side + 1) * LEAF].astype(BF16)
+        wide[count + 2 + side] = high[:, side * LEAF : (side + 1) * LEAF].astype(BF16)
+
+    def body(step, carry):
+        load(step).wait()
+        for item in range(per):
+            box = step * per + item
+            left = jnp.concatenate([wide[index[box * 3 + side]] for side in range(3)], axis=1)
+            right = jnp.concatenate([blocks[box, side] for side in range(3)], axis=1)
+            at = pl.ds(pl.multiple_of(box * LEAF, LEAF), LEAF)
+            total[:, at] = lax.dot_general(left, right, NT, preferred_element_type=F32)
+        store(step).start()
+        return carry
+
+    lax.fori_loop(0, NEAR_STEPS, body, 0)
+    for step in range(NEAR_STEPS):
+        store(step).wait()
 
 
 def near_field(index, blocks, boxes, low, high):
     count = blocks.shape[0]
-    per = 8
+    vmem = pl.BlockSpec(memory_space=pltpu.VMEM)
+    anywhere = pl.BlockSpec(memory_space=pl.ANY)
     return pl.pallas_call(
         near_kernel,
-        grid_spec=pltpu.PrefetchScalarGridSpec(
-            num_scalar_prefetch=1,
-            grid=(count // per,),
-            in_specs=[
-                pl.BlockSpec((per, 3, LEAF, LEAF), lambda i, s: (i, 0, 0, 0)),
-                pl.BlockSpec((count, COLS, LEAF), lambda i, s: (0, 0, 0)),
-                pl.BlockSpec((COLS, 2 * LEAF), lambda i, s: (0, 0)),
-                pl.BlockSpec((COLS, 2 * LEAF), lambda i, s: (0, 0)),
-            ],
-            out_specs=pl.BlockSpec((COLS, per * LEAF), lambda i, s: (0, i)),
-            scratch_shapes=[pltpu.VMEM((count + 4, COLS, LEAF), BF16)],
-        ),
+        in_specs=[pl.BlockSpec(memory_space=pltpu.SMEM), anywhere, vmem, vmem, vmem],
+        out_specs=anywhere,
         out_shape=jax.ShapeDtypeStruct((COLS, count * LEAF), F32),
+        scratch_shapes=[
+            pltpu.VMEM((count + 4, COLS, LEAF), BF16),
+            pltpu.VMEM(blocks.shape, BF16),
+            pltpu.VMEM((COLS, count * LEAF), F32),
+            pltpu.SemaphoreType.DMA((2, NEAR_STEPS)),
+        ],
         compiler_params=pltpu.CompilerParams(vmem_limit_bytes=56 * 2**20),
         cost_estimate=pl.CostEstimate(
             flops=5 * 10**8, bytes_accessed=16 * 10**6, transcendentals=0
@@ -280,7 +294,7 @@
     )(index, blocks, boxes, low, high)
 
 
-def inner_kernel(side, arrived, factors_hbm, out, factors, stage, high0, low0, high1, low1, sems):
+def inner_kernel(side, arrived, factors_hbm, own, sent, factors, stage, high0, low0, high1, low1, sems):
     levels = factors.shape[0]
     sources = arrived.shape[0] // 16
 
@@ -294,14 +308,14 @@
     for first in range(0, sources, 8):
         both = [arrived[pl.ds((first + i) * 16, 16), :].astype(F32) for i in range(8)]
         for which in range(2):
-            sent = [value[which * 8 : which * 8 + 8] for value in both]
+            message = [value[which * 8 : which * 8 + 8] for value in both]
             for kid in range(2):
                 parts = []
                 for part in range(4):
                     lines = []
                     for i in range(4):
                         shift = (i - part) * 32 % 128
-                        value = sent[kid + 2 * i]
+                        value = message[kid + 2 * i]
                         lines.append(pltpu.roll(value, shift, 1) if shift else value)
                     parts.append(pick(lines))
                 high0[which, first // 4 + kid] = jnp.concatenate(parts, axis=0).astype(BF16)
@@ -322,8 +336,8 @@
     level_copy(levels - 1).wait()
     last = factors.at[levels - 1]
     run_level(level_step(levels - 1), NATURAL, last, odd, even, stage)
-    for which in range(2):
-        out[which ^ side[0]] = high0[which]
+    own[...] = high0[side[0]]
+    sent[...] = high0[1 - side[0]]
 
 
 def inner(side, arrived, factors):
@@ -336,8 +350,8 @@
             pl.BlockSpec(memory_space=pltpu.VMEM),
             pl.BlockSpec(memory_space=pl.ANY),
         ],
-        out_specs=pl.BlockSpec(memory_space=pltpu.VMEM),
-        out_shape=jax.ShapeDtypeStruct((2, sources // 4, RANK, 128), BF16),
+        out_specs=[pl.BlockSpec(memory_space=pltpu.VMEM)] * 2,
+        out_shape=[jax.ShapeDtypeStruct((sources // 4, RANK, 128), BF16)] * 2,
         scratch_shapes=[
             pltpu.VMEM(factors.shape, BF16),
             pltpu.VMEM((sources // 4, 256, 128), F32),
@@ -347,7 +361,7 @@
             state,
             pltpu.SemaphoreType.DMA((levels,)),
         ],
-        compiler_params=pltpu.CompilerParams(vmem_limit_bytes=56 * 2**20),
+        compiler_params=pltpu.CompilerParams(vmem_limit_bytes=16 * 2**20),
         cost_estimate=pl.CostEstimate(
             flops=2 * 10**8, bytes_accessed=2 * 10**6, transcendentals=0
         ),
@@ -355,37 +369,67 @@
     )(side, arrived, factors)
 
 
-def expand_kernel(side, coeffs, expand, near, out):
-    for quad in range(coeffs.shape[0]):
-        turned = coeffs[quad].astype(F32).T.astype(BF16)
-        for part in range(4):
-            box = quad * 4 + part
-            value = jnp.dot(
-                turned[part * COLS : (part + 1) * COLS],
+EXPAND_STEPS = 4
+
+
+def expand_kernel(side, coeffs, expand_hbm, near_hbm, out_hbm, expand, near, sems):
+    boxes = expand.shape[0]
+    per = boxes // EXPAND_STEPS
+    width = per * LEAF
+
+    def block(step):
+        return pl.ds(pl.multiple_of(side[0] * (boxes * LEAF) + step * width, LEAF), width)
+
+    def loads(step):
+        at = pl.ds(step * per, per)
+        here = pl.ds(step * width, width)
+        return (
+            pltpu.make_async_copy(expand_hbm.at[at], expand.at[at], sems.at[0, step]),
+            pltpu.make_async_copy(near_hbm.at[:, block(step)], near.at[:, here], sems.at[1, step]),
+        )
+
+    def store(step):
+        here = pl.ds(step * width, width)
+        return pltpu.make_async_copy(near.at[:, here], out_hbm.at[:, block(step)], sems.at[2, step])
+
+    for step in range(EXPAND_STEPS):
+        for copy in loads(step):
+            copy.start()
+    turned = [coeffs[quad].astype(F32).T.astype(BF16) for quad in range(boxes // 4)]
+    for step in range(EXPAND_STEPS):
+        for copy in loads(step):
+            copy.wait()
+        for box in range(step * per, (step + 1) * per):
+            part = box % 4
+            at = pl.ds(box * LEAF, LEAF)
+            near[:, at] += jnp.dot(
+                turned[box // 4][part * COLS : (part + 1) * COLS],
                 expand[box],
                 preferred_element_type=F32,
             )
-            at = pl.ds(box * LEAF, LEAF)
-            out[:, at] = near[:, at] + value
+        store(step).start()
+    for step in range(EXPAND_STEPS):
+        store(step).wait()
 
 
 def expand_into(side, coeffs, expand, near):
     boxes = expand.shape[0]
-    steps = 4
-    per = boxes // steps
+    anywhere = pl.BlockSpec(memory_space=pl.ANY)
     return pl.pallas_call(
         expand_kernel,
-        grid_spec=pltpu.PrefetchScalarGridSpec(
-            num_scalar_prefetch=1,
-            grid=(steps,),
-            in_specs=[
-                pl.BlockSpec((per // 4, RANK, 128), lambda i, s: (i, 0, 0)),
-                pl.BlockSpec((per, RANK, LEAF), lambda i, s: (i, 0, 0)),
-                pl.BlockSpec((COLS, per * LEAF), lambda i, s: (0, s[0] * steps + i)),
-            ],
-            out_specs=pl.BlockSpec((COLS, per * LEAF), lambda i, s: (0, s[0] * steps + i)),
-        ),
+        in_specs=[
+            pl.BlockSpec(memory_space=pltpu.SMEM),
+            pl.BlockSpec(memory_space=pltpu.VMEM),
+            anywhere,
+            anywhere,
+        ],
+        out_specs=anywhere,
         out_shape=jax.ShapeDtypeStruct(near.shape, F32),
+        scratch_shapes=[
+            pltpu.VMEM(expand.shape, BF16),
+            pltpu.VMEM((COLS, boxes * LEAF), F32),
+            pltpu.SemaphoreType.DMA((3, EXPAND_STEPS)),
+        ],
         input_output_aliases={3: 0},
         compiler_params=pltpu.CompilerParams(vmem_limit_bytes=8 * 2**20),
         cost_estimate=pl.CostEstimate(
@@ -409,21 +453,20 @@
     low = lax.ppermute(rhs_vectors[:, -width:], "blk", forward)
     high = lax.ppermute(rhs_vectors[:, :width], "blk", backward)
 
+    boxes, outgoing = outer(rhs_vectors, leaf_basis, outer_levels)
+    outgoing, low, high, own_expand = lax.optimization_barrier((outgoing, low, high, leaf_expand))
+    other_expand = lax.ppermute(own_expand, "rhs", swap)
     total_boxes = box_count * blocks
     first_box = lax.axis_index("blk") * box_count
     local = jnp.arange(box_count, dtype=jnp.int32)
     offsets = jnp.mod(near_list - (first_box + local)[:, None] + total_boxes // 2, total_boxes)
     index = (local[:, None] + 2 + offsets - total_boxes // 2).reshape(-1)
-
-    boxes, outgoing = outer(rhs_vectors, leaf_basis, outer_levels)
-    outgoing, low, high, own_expand = lax.optimization_barrier((outgoing, low, high, leaf_expand))
-    other_expand = lax.ppermute(own_expand, "rhs", swap)
     arrived = lax.all_to_all(outgoing, ("blk", "rhs"), split_axis=0, concat_axis=0, tiled=True)
     near = near_field(index, near_blocks, boxes, low, high)
     arrived, near = lax.optimization_barrier((arrived, near))
-    coeffs = inner(side, arrived, inner_levels)
-    other = lax.ppermute(coeffs[1], "rhs", swap)
-    result = expand_into(side, coeffs[0], leaf_expand, near)
+    own, sent = inner(side, arrived, inner_levels)
+    other = lax.ppermute(sent, "rhs", swap)
+    result = expand_into(side, own, leaf_expand, near)
     return expand_into(1 - side, other, other_expand, result)
 
 

time: 59.8 us -> 49.5 us (0.83); the launches traced: 58.9 us -> 49.2 us
  Pallas kernels: 39.9 us -> 29.9 us
  local copies, waits for them, and re-layouts: 3.39 us -> 1.7 us
  waiting for transfers between devices: 0.49 us -> 1.97 us
    pallas_call x3, Pallas kernels: 23 us -> 15.2 us  [the longest x1 9.77 us: near_field(): pl.pallas_call(near_kernel, in_specs=[pl.BlockSpec(memory_space=pltpu.SME...]
    pallas_call x1, Pallas kernels: 7.63 us -> 5.41 us  [inner(): pl.pallas_call(inner_kernel, in_specs=[pl.BlockSpec(memory_space=pltpu.SM...]
    squeeze x1 -> x0, local copies, waits for them, and re-layouts: 0.99 us -> none  [shards(): result = expand_into(side, coeffs[0], leaf_expand, near)]
    ppermute x1, waiting for transfers between devices: 0.48 us -> 1.25 us  [shards(): other = lax.ppermute(sent, 'rhs', swap)]
    all_to_all x1, waiting for transfers between devices: 0.01 us -> 0.71 us  [shards(): lax.all_to_all(outgoing, ('blk', 'rhs'), split_axis=0, concat_axis=0, til...]
    unnamed x10, local copies, waits for them, and re-layouts: 0.72 us -> 0.02 us
    ppermute x1, starting transfers between devices: 0.16 us -> 0.79 us  [shards(): other = lax.ppermute(sent, 'rhs', swap)]
  transfers between devices with their start and end apart: 5 -> 5, of which waited for: 1 -> 2; matrix products, arithmetic and copies ran while one was open for 3% -> 2% of each run, Pallas kernels for 61% -> 55%
where the time goes in v2:
time: 49.5 us; the launch traced here: 49.2 us
  Pallas kernels  29.9 us (60%)
  starting transfers between devices  15.5 us (31%)
  waiting for transfers between devices  1.97 us (4%)
  local copies, waits for them, and re-layouts  1.7 us (3%)
    all_to_all x1, starting transfers between devices, shards(): lax.all_to_all(outgoing, ('blk', 'rhs'), split_axis=0, concat_axis=0, til...  10.3 us
    pallas_call x1, Pallas kernels, near_field(): pl.pallas_call(near_kernel, in_specs=[pl.BlockSpec(memory_space=pltpu.SME...  9.77 us
    pallas_call x1, Pallas kernels, outer(): pl.pallas_call(outer_kernel, in_specs=[whole, whole, whole], out_specs=[p...  9.27 us
    pallas_call x2, Pallas kernels, expand_into(): pl.pallas_call(expand_kernel, in_specs=[pl.BlockSpec(memory_space=pltpu.S...  5.45 us
    pallas_call x1, Pallas kernels, inner(): pl.pallas_call(inner_kernel, in_specs=[pl.BlockSpec(memory_space=pltpu.SM...  5.41 us
    ppermute x1, starting transfers between devices, shards(): low = lax.ppermute(rhs_vectors[:, -width:], 'blk', forward)  3.03 us
    ppermute x1, starting transfers between devices, shards(): other_expand = lax.ppermute(own_expand, 'rhs', swap)  1.38 us
    ppermute x1, waiting for transfers between devices, shards(): other = lax.ppermute(sent, 'rhs', swap)  1.25 us
  transfers between devices with their start and end apart: 5, of which 2 were waited for; matrix products, arithmetic and copies ran while one was open for 2% of the time, Pallas kernels for 55%

profile of v2, /device:TPU:1, one launch (start us, length us, event | category | flops | bytes accessed | tf_op | source)
XLA Modules:
  0.0 49.2 jit_solution(414159143871456322)
XLA Ops:
  0.0 0.8 %fusion.3 = (f32[32,256]{1,0:T(8,128)S(1)}, f32[32,256]{1,0:T(8,128)S(1)}) fusion(f32[32,16384]{1,0:T(8,128)} %rhs_hbm.1), kind=kLoop, calls=%fused_computation.8 | loop fusion | bytes 131072 | tf_op jit(solution)/shard_map/slice | solution.py:454
  0.8 3.0 %collective-permute-start = (f32[32,256]{1,0:T(8,128)S(1)}, f32[32,256]{1,0:T(8,128)S(1)}, u32[]{:S(2)}, u32[]{:S(2)}) collective-permute-start(f32[32,256]{1,0:T(8,128)S(1)} %get-tuple-element.26), channel_id=1, source_target_pairs={{0,2},{2,4},{4,6},{6,8},{8,10},{10,12},{12,14},{14,16},{16,18},{18... | collective-permute-start | bytes 98312 | tf_op jit(solution)/shard_map/ppermute | solution.py:453
  3.8 0.0 collective-permute-start.1
  3.8 0.0 copy-start.1
  3.8 0.0 copy-start.4
  3.8 9.3 %outer_levels.1 = (bf16[128,32,128]{2,1,0:T(8,128)(2,1)}, bf16[1024,128]{1,0:T(8,128)(2,1)}) custom-call(f32[32,16384]{1,0:T(8,128)} %rhs_hbm.1, bf16[128,32,128]{2,1,0:T(8,128)(2,1)} %basis_hbm.1, bf16[7,128,2048]{2,1,0:T(8,128)(2,1)} %factors_hbm.2), custom_call_target="tpu_custom_call" | custom-call | flops 400000000 | bytes 8000000 | tf_op jit(solution)/shard_map/outer_levels/pallas_call | solution.py:209
  13.1 0.0 collective-permute-done.low
  13.1 0.0 copy-start.2
  13.1 0.0 collective-permute-done.1.high
  13.1 0.0 copy-start.3
  13.1 0.0 copy-done.1
  13.1 1.4 %collective-permute-start.3 = (bf16[64,32,128]{2,1,0:T(8,128)(2,1)S(1)}, bf16[64,32,128]{2,1,0:T(8,128)(2,1)S(1)}, u32[]{:S(2)}, u32[]{:S(2)}) collective-permute-start(bf16[64,32,128]{2,1,0:T(8,128)(2,1)S(1)} %copy-done.1), channel_id=1, source_target_pairs={{0,1},{1,0},{2,3},{3,2},{4,5},{5,4},{6,7},{7,6},{8,9},{9,8},{10,11... | collective-permute-start | bytes 1572872 | tf_op jit(solution)/shard_map/ppermute | solution.py:458
  14.5 10.3 %all-to-all-start = ((bf16[128,8,128]{2,1,0:T(8,128)(2,1)}), bf16[128,8,128]{2,1,0:T(8,128)(2,1)S(1)}, u32[]{:S(2)}, u32[]{:S(2)}) async-start(bf16[128,8,128]{2,1,0:T(8,128)(2,1)} %bitcast.4), calls=%async_computation | async-start | bytes 524288 | tf_op jit(solution)/shard_map/all_to_all | solution.py:464
  24.9 0.0 copy-done.4
  24.9 0.1 copy.10
  25.0 0.8 %reshape.18.index = s32[384]{0:T(512)} reshape(s32[128,3]{1,0:T(8,128)S(1)} %copy.10) | data formatting | bytes 3072 | tf_op jit(solution)/shard_map/reshape | solution.py:463
  25.8 0.0 copy-done.2
  25.8 0.0 copy-done.3
  25.8 0.0 copy-start
  25.8 9.8 %near_field.1.near_hbm = f32[32,16384]{1,0:T(8,128)} custom-call(s32[384]{0:T(512)} %reshape.18.index, bf16[128,3,128,128]{3,2,1,0:T(8,128)(2,1)} %blocks_hbm.1, bf16[128,32,128]{2,1,0:T(8,128)(2,1)} %get-tuple-element.17.boxes, f32[32,256]{1,0:T(8,128)} %copy-done.2, f32[32,256]{1,0:T(8,128)} %copy-done.3), custom_call_target="tpu_custom_call" | custom-call | flops 500000000 | bytes 16000000 | tf_op jit(solution)/shard_map/near_field/pallas_call | solution.py:278
  35.6 0.7 %all-to-all-done = bf16[128,8,128]{2,1,0:T(8,128)(2,1)S(1)} async-done(((bf16[128,8,128]{2,1,0:T(8,128)(2,1)}), bf16[128,8,128]{2,1,0:T(8,128)(2,1)S(1)}, u32[]{:S(2)}, u32[]{:S(2)}) %all-to-all-start) | async-done | bytes 262176 | tf_op jit(solution)/shard_map/all_to_all | solution.py:464
  36.3 0.0 copy-done
  36.3 5.4 %inner_levels.1 = (bf16[16,32,128]{2,1,0:T(8,128)(2,1)S(1)}, bf16[16,32,128]{2,1,0:T(8,128)(2,1)S(1)}) custom-call(s32[1]{0:T(128)} %bitcast.side, bf16[1024,128]{1,0:T(8,128)(2,1)S(1)} %bitcast.3, bf16[6,64,2048]{2,1,0:T(8,128)(2,1)S(1)} %copy-done), custom_call_target="tpu_custom_call" | custom-call | flops 200000000 | bytes 2000000 | tf_op jit(solution)/shard_map/inner_levels/pallas_call | solution.py:346
  41.7 0.8 %collective-permute-start.2 = (bf16[16,32,128]{2,1,0:T(8,128)(2,1)S(1)}, bf16[16,32,128]{2,1,0:T(8,128)(2,1)S(1)}, u32[]{:S(2)}, u32[]{:S(2)}) collective-permute-start(bf16[16,32,128]{2,1,0:T(8,128)(2,1)S(1)} %get-tuple-element.21), channel_id=1, source_target_pairs={{0,1},{1,0},{2,3},{3,2},{4,5},{5,4},{6,7},{7,6},{8,9},{9,8},{10,11... | collective-permute-start | bytes 393224 | tf_op jit(solution)/shard_map/ppermute | solution.py:468
  42.5 2.7 %expand_boxes.2.near_hbm = f32[32,16384]{1,0:T(8,128)} custom-call(s32[1]{0:T(128)} %bitcast.side, bf16[16,32,128]{2,1,0:T(8,128)(2,1)S(1)} %get-tuple-element.23.coeffs, bf16[64,32,128]{2,1,0:T(8,128)(2,1)S(1)} %copy-done.1, f32[32,16384]{1,0:T(8,128)} %near_field.1.near_hbm), custom_call_target="tpu_custom_call", output_to_operand_aliasing={{}: (3, {})} | custom-call | flops 20000000 | bytes 3000000 | tf_op jit(solution)/shard_map/expand_boxes/pallas_call | solution.py:418
  45.2 1.2 %collective-permute-done.2.coeffs = bf16[16,32,128]{2,1,0:T(8,128)(2,1)S(1)} collective-permute-done((bf16[16,32,128]{2,1,0:T(8,128)(2,1)S(1)}, bf16[16,32,128]{2,1,0:T(8,128)(2,1)S(1)}, u32[]{:S(2)}, u32[]{:S(2)}) %collective-permute-start.2) | collective-permute-done | bytes 131104 | tf_op jit(solution)/shard_map/ppermute | solution.py:468
  46.5 0.0 collective-permute-done.3.expand_hbm
  46.5 2.7 %expand_boxes.3 = f32[32,16384]{1,0:T(8,128)} custom-call(s32[1]{0:T(128)S(6)} %sub.14.side, bf16[16,32,128]{2,1,0:T(8,128)(2,1)S(1)} %collective-permute-done.2.coeffs, bf16[64,32,128]{2,1,0:T(8,128)(2,1)S(1)} %collective-permute-done.3.expand_hbm, f32[32,16384]{1,0:T(8,128)} %expand_boxes.2.near_hbm), custom_call_target="tpu_custom_call", output_to_operand_aliasing={{}: (3, {})} | custom-call | flops 20000000 | bytes 3000000 | tf_op jit(solution)/shard_map/expand_boxes/pallas_call | solution.py:418
  (2 shorter events, 0.0 us)
Async XLA Ops:
  0.8 12.3 %collective-permute-start = (f32[32,256]{1,0:T(8,128)S(1)}, f32[32,256]{1,0:T(8,128)S(1)}, u32[]{:S(2)}, u32[]{:S(2)}) collective-permute-start(f32[32,256]{1,0:T(8,128)S(1)} %get-tuple-element.26), channel_id=1, source_target_pairs={{0,2},{2,4},{4,6},{6,8},{8,10},{10,12},{12,14},{14,16},{16,18},{18... | collective-permute-start | bytes 98312 | tf_op jit(solution)/shard_map/ppermute | solution.py:453
  3.8 9.3 %collective-permute-start.1 = (f32[32,256]{1,0:T(8,128)S(1)}, f32[32,256]{1,0:T(8,128)S(1)}, u32[]{:S(2)}, u32[]{:S(2)}) collective-permute-start(f32[32,256]{1,0:T(8,128)S(1)} %get-tuple-element.25), channel_id=1, source_target_pairs={{0,126},{2,0},{4,2},{6,4},{8,6},{10,8},{12,10},{14,12},{16,14},{18... | collective-permute-start | bytes 98312 | tf_op jit(solution)/shard_map/ppermute | solution.py:454
  3.8 9.3 %copy-start.1 = (bf16[64,32,128]{2,1,0:T(8,128)(2,1)S(1)}, bf16[64,32,128]{2,1,0:T(8,128)(2,1)}, u32[]{:S(2)}) copy-start(bf16[64,32,128]{2,1,0:T(8,128)(2,1)} %expand_hbm.1) | copy-start | bytes 1572868
  3.8 21.1 %copy-start.4 = (s32[128,3]{0,1:T(4,128)S(1)}, s32[128,3]{0,1:T(4,128)}, u32[]{:S(2)}) copy-start(s32[128,3]{0,1:T(4,128)} %param.13) | copy-start | bytes 4612
  13.1 12.7 %copy-start.2 = (f32[32,256]{1,0:T(8,128)}, f32[32,256]{1,0:T(8,128)S(1)}, u32[]{:S(2)}) copy-start(f32[32,256]{1,0:T(8,128)S(1)} %collective-permute-done.low) | copy-start | bytes 98308
  13.1 12.7 %copy-start.3 = (f32[32,256]{1,0:T(8,128)}, f32[32,256]{1,0:T(8,128)S(1)}, u32[]{:S(2)}) copy-start(f32[32,256]{1,0:T(8,128)S(1)} %collective-permute-done.1.high) | copy-start | bytes 98308
  13.1 33.3 %collective-permute-start.3 = (bf16[64,32,128]{2,1,0:T(8,128)(2,1)S(1)}, bf16[64,32,128]{2,1,0:T(8,128)(2,1)S(1)}, u32[]{:S(2)}, u32[]{:S(2)}) collective-permute-start(bf16[64,32,128]{2,1,0:T(8,128)(2,1)S(1)} %copy-done.1), channel_id=1, source_target_pairs={{0,1},{1,0},{2,3},{3,2},{4,5},{5,4},{6,7},{7,6},{8,9},{9,8},{10,11... | collective-permute-start | bytes 1572872 | tf_op jit(solution)/shard_map/ppermute | solution.py:458
  14.5 21.8 %all-to-all-start = ((bf16[128,8,128]{2,1,0:T(8,128)(2,1)}), bf16[128,8,128]{2,1,0:T(8,128)(2,1)S(1)}, u32[]{:S(2)}, u32[]{:S(2)}) async-start(bf16[128,8,128]{2,1,0:T(8,128)(2,1)} %bitcast.4), calls=%async_computation | async-start | bytes 524288 | tf_op jit(solution)/shard_map/all_to_all | solution.py:464
  25.8 10.5 %copy-start = (bf16[6,64,2048]{2,1,0:T(8,128)(2,1)S(1)}, bf16[6,64,2048]{2,1,0:T(8,128)(2,1)}, u32[]{:S(2)}) copy-start(bf16[6,64,2048]{2,1,0:T(8,128)(2,1)} %factors_hbm.3) | copy-start | bytes 4718596
  41.7 4.8 %collective-permute-start.2 = (bf16[16,32,128]{2,1,0:T(8,128)(2,1)S(1)}, bf16[16,32,128]{2,1,0:T(8,128)(2,1)S(1)}, u32[]{:S(2)}, u32[]{:S(2)}) collective-permute-start(bf16[16,32,128]{2,1,0:T(8,128)(2,1)S(1)} %get-tuple-element.21), channel_id=1, source_target_pairs={{0,1},{1,0},{2,3},{3,2},{4,5},{5,4},{6,7},{7,6},{8,9},{9,8},{10,11... | collective-permute-start | bytes 393224 | tf_op jit(solution)/shard_map/ppermute | solution.py:468

commit v3 on v2

--- a/solution.py
+++ b/solution.py
@@ -257,12 +257,25 @@
 
     def body(step, carry):
         load(step).wait()
-        for item in range(per):
-            box = step * per + item
-            left = jnp.concatenate([wide[index[box * 3 + side]] for side in range(3)], axis=1)
-            right = jnp.concatenate([blocks[box, side] for side in range(3)], axis=1)
-            at = pl.ds(pl.multiple_of(box * LEAF, LEAF), LEAF)
-            total[:, at] = lax.dot_general(left, right, NT, preferred_element_type=F32)
+        zero = jnp.zeros((COLS, LEAF), BF16)
+        for item in range(0, per, 2):
+            pair = (step * per + item, step * per + item + 1)
+            last = [wide[index[2, box]] for box in pair]
+            left = jnp.concatenate(
+                [
+                    jnp.concatenate([last[0], zero], axis=1),
+                    jnp.concatenate([zero, last[1]], axis=1),
+                ],
+                axis=0,
+            )
+            right = jnp.concatenate([blocks[box, 2] for box in pair], axis=1)
+            third = lax.dot_general(left, right, NT, preferred_element_type=F32)
+            for side, box in enumerate(pair):
+                left = jnp.concatenate([wide[index[0, box]], wide[index[1, box]]], axis=1)
+                right = jnp.concatenate([blocks[box, 0], blocks[box, 1]], axis=1)
+                value = lax.dot_general(left, right, NT, preferred_element_type=F32)
+                at = pl.ds(pl.multiple_of(box * LEAF, LEAF), LEAF)
+                total[:, at] = value + third[side * COLS : (side + 1) * COLS]
         store(step).start()
         return carry
 
@@ -459,8 +472,8 @@
     total_boxes = box_count * blocks
     first_box = lax.axis_index("blk") * box_count
     local = jnp.arange(box_count, dtype=jnp.int32)
-    offsets = jnp.mod(near_list - (first_box + local)[:, None] + total_boxes // 2, total_boxes)
-    index = (local[:, None] + 2 + offsets - total_boxes // 2).reshape(-1)
+    offsets = jnp.mod(near_list.T - (first_box + local) + total_boxes // 2, total_boxes)
+    index = local + 2 + offsets - total_boxes // 2
     arrived = lax.all_to_all(outgoing, ("blk", "rhs"), split_axis=0, concat_axis=0, tiled=True)
     near = near_field(index, near_blocks, boxes, low, high)
     arrived, near = lax.optimization_barrier((arrived, near))

time: 49.5 us -> 49.5 us (level)
  waiting for transfers between devices: 1.97 us -> 3.09 us
  local copies, waits for them, and re-layouts: 1.7 us -> 0.8 us
  other arithmetic: 0.02 us -> 0.59 us
    reshape x1 -> x0, local copies, waits for them, and re-layouts: 0.78 us -> none  [shards(): index = (local[:, None] + 2 + offsets - total_boxes // 2).reshape(-1)]
    all_to_all x1, waiting for transfers between devices: 0.71 us -> 1.48 us  [shards(): lax.all_to_all(outgoing, ('blk', 'rhs'), split_axis=0, concat_axis=0, til...]
    sub x1, other arithmetic: 0.01 us -> 0.59 us  [shards(): index = local + 2 + offsets - total_boxes // 2]
  transfers between devices with their start and end apart: 5 -> 5, of which waited for: 2 -> 2; matrix products, arithmetic and copies ran while one was open for 2% -> 1% of each run, Pallas kernels for 55% -> 54%
where the time goes in v3:
time: 49.5 us; the launch traced here: 49.2 us
  Pallas kernels  29.5 us (60%)
  starting transfers between devices  15.2 us (31%)
  waiting for transfers between devices  3.09 us (6%)
  local copies, waits for them, and re-layouts  0.8 us (2%)
  other arithmetic  0.59 us (1%)
    all_to_all x1, starting transfers between devices, shards(): lax.all_to_all(outgoing, ('blk', 'rhs'), split_axis=0, concat_axis=0, til...  10.3 us
    pallas_call x1, Pallas kernels, near_field(): pl.pallas_call(near_kernel, in_specs=[pl.BlockSpec(memory_space=pltpu.SME...  9.33 us
    pallas_call x1, Pallas kernels, outer(): pl.pallas_call(outer_kernel, in_specs=[whole, whole, whole], out_specs=[p...  9.27 us
    pallas_call x2, Pallas kernels, expand_into(): pl.pallas_call(expand_kernel, in_specs=[pl.BlockSpec(memory_space=pltpu.S...  5.45 us
    pallas_call x1, Pallas kernels, inner(): pl.pallas_call(inner_kernel, in_specs=[pl.BlockSpec(memory_space=pltpu.SM...  5.41 us
    ppermute x1, starting transfers between devices, shards(): low = lax.ppermute(rhs_vectors[:, -width:], 'blk', forward)  3.03 us
    ppermute x1, waiting for transfers between devices, shards(): other = lax.ppermute(sent, 'rhs', swap)  1.6 us
    all_to_all x1, waiting for transfers between devices, shards(): lax.all_to_all(outgoing, ('blk', 'rhs'), split_axis=0, concat_axis=0, til...  1.48 us
  transfers between devices with their start and end apart: 5, of which 2 were waited for; matrix products, arithmetic and copies ran while one was open for 1% of the time, Pallas kernels for 54%

profile of v3, /device:TPU:1, one launch (start us, length us, event | category | flops | bytes accessed | tf_op | source)
XLA Modules:
  0.0 49.2 jit_solution(15760271764605743908)
XLA Ops:
  0.0 0.8 %fusion.3 = (f32[32,256]{1,0:T(8,128)S(1)}, f32[32,256]{1,0:T(8,128)S(1)}) fusion(f32[32,16384]{1,0:T(8,128)} %rhs_hbm.1), kind=kLoop, calls=%fused_computation.8 | loop fusion | bytes 131072 | tf_op jit(solution)/shard_map/slice | solution.py:467
  0.8 3.0 %collective-permute-start = (f32[32,256]{1,0:T(8,128)S(1)}, f32[32,256]{1,0:T(8,128)S(1)}, u32[]{:S(2)}, u32[]{:S(2)}) collective-permute-start(f32[32,256]{1,0:T(8,128)S(1)} %get-tuple-element.26), channel_id=1, source_target_pairs={{0,2},{2,4},{4,6},{6,8},{8,10},{10,12},{12,14},{14,16},{16,18},{18... | collective-permute-start | bytes 98312 | tf_op jit(solution)/shard_map/ppermute | solution.py:466
  3.8 0.0 collective-permute-start.1
  3.8 0.0 copy-start.1
  3.8 0.0 copy-start.4
  3.8 9.3 %outer_levels.1 = (bf16[128,32,128]{2,1,0:T(8,128)(2,1)}, bf16[1024,128]{1,0:T(8,128)(2,1)}) custom-call(f32[32,16384]{1,0:T(8,128)} %rhs_hbm.1, bf16[128,32,128]{2,1,0:T(8,128)(2,1)} %basis_hbm.1, bf16[7,128,2048]{2,1,0:T(8,128)(2,1)} %factors_hbm.2), custom_call_target="tpu_custom_call" | custom-call | flops 400000000 | bytes 8000000 | tf_op jit(solution)/shard_map/outer_levels/pallas_call | solution.py:209
  13.1 0.0 collective-permute-done.low
  13.1 0.0 copy-start.2
  13.1 0.0 collective-permute-done.1.high
  13.1 0.0 copy-start.3
  13.1 0.0 copy-done.1
  13.1 1.4 %collective-permute-start.3 = (bf16[64,32,128]{2,1,0:T(8,128)(2,1)S(1)}, bf16[64,32,128]{2,1,0:T(8,128)(2,1)S(1)}, u32[]{:S(2)}, u32[]{:S(2)}) collective-permute-start(bf16[64,32,128]{2,1,0:T(8,128)(2,1)S(1)} %copy-done.1), channel_id=1, source_target_pairs={{0,1},{1,0},{2,3},{3,2},{4,5},{5,4},{6,7},{7,6},{8,9},{9,8},{10,11... | collective-permute-start | bytes 1572872 | tf_op jit(solution)/shard_map/ppermute | solution.py:471
  14.5 10.3 %all-to-all-start = ((bf16[128,8,128]{2,1,0:T(8,128)(2,1)}), bf16[128,8,128]{2,1,0:T(8,128)(2,1)S(1)}, u32[]{:S(2)}, u32[]{:S(2)}) async-start(bf16[128,8,128]{2,1,0:T(8,128)(2,1)} %bitcast.8), calls=%async_computation | async-start | bytes 524288 | tf_op jit(solution)/shard_map/all_to_all | solution.py:477
  24.9 0.0 copy-done.4
  24.9 0.6 %fusion.2.index = s32[3,128]{1,0:T(4,128)} fusion(s32[128,3]{0,1:T(4,128)S(1)} %copy-done.4, s32[128]{0:T(128)S(1)} %get-tuple-element.27, s32[128]{0:T(128)S(1)} %get-tuple-element.28), kind=kLoop, calls=%fused_computation.5 | loop fusion | flops 5760 | bytes 4096 | tf_op jit(solution)/shard_map/sub | solution.py:476
  25.5 0.0 copy-done.2
  25.5 0.0 copy-done.3
  25.5 0.0 copy-start
  25.5 9.3 %near_field.1.near_hbm = f32[32,16384]{1,0:T(8,128)} custom-call(s32[3,128]{1,0:T(4,128)} %fusion.2.index, bf16[128,3,128,128]{3,2,1,0:T(8,128)(2,1)} %blocks_hbm.1, bf16[128,32,128]{2,1,0:T(8,128)(2,1)} %get-tuple-element.17.boxes, f32[32,256]{1,0:T(8,128)} %copy-done.2, f32[32,256]{1,0:T(8,128)} %copy-done.3), custom_call_target="tpu_custom_call" | custom-call | flops 500000000 | bytes 16000000 | tf_op jit(solution)/shard_map/near_field/pallas_call | solution.py:291
  34.8 1.5 %all-to-all-done = bf16[128,8,128]{2,1,0:T(8,128)(2,1)S(1)} async-done(((bf16[128,8,128]{2,1,0:T(8,128)(2,1)}), bf16[128,8,128]{2,1,0:T(8,128)(2,1)S(1)}, u32[]{:S(2)}, u32[]{:S(2)}) %all-to-all-start) | async-done | bytes 262176 | tf_op jit(solution)/shard_map/all_to_all | solution.py:477
  36.3 0.0 copy-done
  36.3 5.4 %inner_levels.1 = (bf16[16,32,128]{2,1,0:T(8,128)(2,1)S(1)}, bf16[16,32,128]{2,1,0:T(8,128)(2,1)S(1)}) custom-call(s32[1]{0:T(128)} %bitcast.side, bf16[1024,128]{1,0:T(8,128)(2,1)S(1)} %bitcast.7, bf16[6,64,2048]{2,1,0:T(8,128)(2,1)S(1)} %copy-done), custom_call_target="tpu_custom_call" | custom-call | flops 200000000 | bytes 2000000 | tf_op jit(solution)/shard_map/inner_levels/pallas_call | solution.py:359
  41.7 0.4 collective-permute-start.2
  42.1 2.7 %expand_boxes.2.near_hbm = f32[32,16384]{1,0:T(8,128)} custom-call(s32[1]{0:T(128)} %bitcast.side, bf16[16,32,128]{2,1,0:T(8,128)(2,1)S(1)} %get-tuple-element.23.coeffs, bf16[64,32,128]{2,1,0:T(8,128)(2,1)S(1)} %copy-done.1, f32[32,16384]{1,0:T(8,128)} %near_field.1.near_hbm), custom_call_target="tpu_custom_call", output_to_operand_aliasing={{}: (3, {})} | custom-call | flops 20000000 | bytes 3000000 | tf_op jit(solution)/shard_map/expand_boxes/pallas_call | solution.py:431
  44.9 1.6 %collective-permute-done.2.coeffs = bf16[16,32,128]{2,1,0:T(8,128)(2,1)S(1)} collective-permute-done((bf16[16,32,128]{2,1,0:T(8,128)(2,1)S(1)}, bf16[16,32,128]{2,1,0:T(8,128)(2,1)S(1)}, u32[]{:S(2)}, u32[]{:S(2)}) %collective-permute-start.2) | collective-permute-done | bytes 131104 | tf_op jit(solution)/shard_map/ppermute | solution.py:481
  46.5 0.0 collective-permute-done.3.expand_hbm
  46.5 2.7 %expand_boxes.3 = f32[32,16384]{1,0:T(8,128)} custom-call(s32[1]{0:T(128)S(6)} %sub.15.side, bf16[16,32,128]{2,1,0:T(8,128)(2,1)S(1)} %collective-permute-done.2.coeffs, bf16[64,32,128]{2,1,0:T(8,128)(2,1)S(1)} %collective-permute-done.3.expand_hbm, f32[32,16384]{1,0:T(8,128)} %expand_boxes.2.near_hbm), custom_call_target="tpu_custom_call", output_to_operand_aliasing={{}: (3, {})} | custom-call | flops 20000000 | bytes 3000000 | tf_op jit(solution)/shard_map/expand_boxes/pallas_call | solution.py:431
  (1 shorter events, 0.0 us)
Async XLA Ops:
  0.8 12.3 %collective-permute-start = (f32[32,256]{1,0:T(8,128)S(1)}, f32[32,256]{1,0:T(8,128)S(1)}, u32[]{:S(2)}, u32[]{:S(2)}) collective-permute-start(f32[32,256]{1,0:T(8,128)S(1)} %get-tuple-element.26), channel_id=1, source_target_pairs={{0,2},{2,4},{4,6},{6,8},{8,10},{10,12},{12,14},{14,16},{16,18},{18... | collective-permute-start | bytes 98312 | tf_op jit(solution)/shard_map/ppermute | solution.py:466
  3.8 9.3 %collective-permute-start.1 = (f32[32,256]{1,0:T(8,128)S(1)}, f32[32,256]{1,0:T(8,128)S(1)}, u32[]{:S(2)}, u32[]{:S(2)}) collective-permute-start(f32[32,256]{1,0:T(8,128)S(1)} %get-tuple-element.25), channel_id=1, source_target_pairs={{0,126},{2,0},{4,2},{6,4},{8,6},{10,8},{12,10},{14,12},{16,14},{18... | collective-permute-start | bytes 98312 | tf_op jit(solution)/shard_map/ppermute | solution.py:467
  3.8 9.3 %copy-start.1 = (bf16[64,32,128]{2,1,0:T(8,128)(2,1)S(1)}, bf16[64,32,128]{2,1,0:T(8,128)(2,1)}, u32[]{:S(2)}) copy-start(bf16[64,32,128]{2,1,0:T(8,128)(2,1)} %expand_hbm.1) | copy-start | bytes 1572868
  3.8 21.1 %copy-start.4 = (s32[128,3]{0,1:T(4,128)S(1)}, s32[128,3]{0,1:T(4,128)}, u32[]{:S(2)}) copy-start(s32[128,3]{0,1:T(4,128)} %param.13) | copy-start | bytes 4612
  13.1 12.4 %copy-start.2 = (f32[32,256]{1,0:T(8,128)}, f32[32,256]{1,0:T(8,128)S(1)}, u32[]{:S(2)}) copy-start(f32[32,256]{1,0:T(8,128)S(1)} %collective-permute-done.low) | copy-start | bytes 98308
  13.1 12.3 %copy-start.3 = (f32[32,256]{1,0:T(8,128)}, f32[32,256]{1,0:T(8,128)S(1)}, u32[]{:S(2)}) copy-start(f32[32,256]{1,0:T(8,128)S(1)} %collective-permute-done.1.high) | copy-start | bytes 98308
  13.1 33.3 %collective-permute-start.3 = (bf16[64,32,128]{2,1,0:T(8,128)(2,1)S(1)}, bf16[64,32,128]{2,1,0:T(8,128)(2,1)S(1)}, u32[]{:S(2)}, u32[]{:S(2)}) collective-permute-start(bf16[64,32,128]{2,1,0:T(8,128)(2,1)S(1)} %copy-done.1), channel_id=1, source_target_pairs={{0,1},{1,0},{2,3},{3,2},{4,5},{5,4},{6,7},{7,6},{8,9},{9,8},{10,11... | collective-permute-start | bytes 1572872 | tf_op jit(solution)/shard_map/ppermute | solution.py:471
  14.5 21.8 %all-to-all-start = ((bf16[128,8,128]{2,1,0:T(8,128)(2,1)}), bf16[128,8,128]{2,1,0:T(8,128)(2,1)S(1)}, u32[]{:S(2)}, u32[]{:S(2)}) async-start(bf16[128,8,128]{2,1,0:T(8,128)(2,1)} %bitcast.8), calls=%async_computation | async-start | bytes 524288 | tf_op jit(solution)/shard_map/all_to_all | solution.py:477
  25.5 10.8 %copy-start = (bf16[6,64,2048]{2,1,0:T(8,128)(2,1)S(1)}, bf16[6,64,2048]{2,1,0:T(8,128)(2,1)}, u32[]{:S(2)}) copy-start(bf16[6,64,2048]{2,1,0:T(8,128)(2,1)} %factors_hbm.3) | copy-start | bytes 4718596
  41.7 4.8 %collective-permute-start.2 = (bf16[16,32,128]{2,1,0:T(8,128)(2,1)S(1)}, bf16[16,32,128]{2,1,0:T(8,128)(2,1)S(1)}, u32[]{:S(2)}, u32[]{:S(2)}) collective-permute-start(bf16[16,32,128]{2,1,0:T(8,128)(2,1)S(1)} %get-tuple-element.21), channel_id=1, source_target_pairs={{0,1},{1,0},{2,3},{3,2},{4,5},{5,4},{6,7},{7,6},{8,9},{9,8},{10,11... | collective-permute-start | bytes 393224 | tf_op jit(solution)/shard_map/ppermute | solution.py:481
